TPU v7x, 512 devices: a whole 4x4x16 slice. The times are simulated.
512 devices in a mesh: dx: 16 (over y, z_lo), dy: 32 (over z_hi, x, core).
Axes of the slice: x: 4, y: 4, z: 16 (z_hi: 4, z_lo: 4; z = z_hi * 4 + z_lo), core: 2. Of those that a mesh axis runs over, the one named last changes fastest.
Arguments:
- images: float32 [131072, 1152], P(('dx', 'dy')), may hold values from -1 to 1
- texts: float32 [131072, 1152], P(('dx', 'dy')), may hold values from -1 to 1
- match: int32 [512, 256], P(('dx', 'dy')), may hold values from 0 to 255, each once within a row
- masks: int32 [3], replicated, may hold values from 1 to 256, as said below
Outputs:
- image_grad: float32 [131072, 1152], P(('dx', 'dy'))
- text_grad: float32 [131072, 1152], P(('dx', 'dy'))
- block_loss: float32 [512], P(('dx', 'dy'))
Inputs may be any that keep to these rules, and one draw needn't show every extreme that they name: `masks`: each entry is a power of two below 512 and the entries differ; the first is below 32, the second is 256.
All inputs are finite; a program needn't handle non-finite values.
Results may differ from a plain program's by a relative error of at most 0.0045.
Values may be sent and summed in bfloat16 or wider, within the bound.
A program may use at most 64 MiB of HBM per device.

v0:
```python
from functools import partial

import jax
import jax.numpy as jnp
from jax import lax
from jax.sharding import PartitionSpec as P

ROUNDS = 3


bias_value = -2.0


def for_sending(value):

    def short(part):
        return part.astype(jnp.bfloat16) if part.dtype == jnp.float32 else part

    return jax.tree.map(short, value)


def from_partner(block, axis, bit):
    count = lax.axis_size(axis)
    route = []
    for low in range(count):
        high = low | 1 << bit
        if high != low and high < count:
            route += [(low, high), (high, low)]
    return lax.ppermute(block, axis, route)


def tile_logits(img_block, txt_block):
    return (
        lax.dot_general(
            img_block, txt_block, (((1,), (1,)), ((), ())), preferred_element_type=jnp.float32
        )
        + bias_value
    )


def tile_weights(logits, labels):
    loss = jnp.sum(jax.nn.softplus(-(2.0 * labels - 1.0) * logits))
    g = (jax.nn.sigmoid(logits) - labels).astype(jnp.bfloat16)
    return (g, loss)


def left_product(g, txt_block):
    return jnp.dot(g, txt_block, preferred_element_type=jnp.float32)


def right_product(g, img_block):
    return lax.dot_general(
        g, img_block, (((0,), (0,)), ((), ())), preferred_element_type=jnp.float32
    )


def visit_dy(value, bit):
    return jax.tree.map(
        lambda part, own: part.astype(own.dtype), from_partner(for_sending(value), "dy", bit), value
    )


def visit_dx(value, bit):
    return jax.tree.map(
        lambda part, own: part.astype(own.dtype), from_partner(for_sending(value), "dx", bit), value
    )


def back_dy(value, bit):
    return from_partner(value, "dy", bit)


def back_dx(value, bit):
    return from_partner(value, "dx", bit)


def route(value, bit_index, low_fn, high_fn, low_bits, high_bits):
    branches = [partial(low_fn, bit=k) for k in range(low_bits)] + [
        partial(high_fn, bit=k) for k in range(high_bits)
    ]
    return lax.switch(bit_index, branches, value)


def body(images, texts, match, masks):
    img = images.astype(jnp.bfloat16)
    txt = texts.astype(jnp.bfloat16)
    rows = img.shape[0]
    column = lax.broadcasted_iota(jnp.int32, (rows, rows), 1)
    labels = (column == match[0][:, None]).astype(jnp.float32)
    logits = tile_logits(img, txt)
    g, total_loss = tile_weights(logits, labels)
    image_grad = left_product(g, txt)
    text_grad = right_product(g, img)
    low_bits = lax.axis_size("dy").bit_length() - 1
    high_bits = lax.axis_size("dx").bit_length() - 1
    zeros = jnp.zeros((rows, rows), jnp.float32)
    for r in range(ROUNDS):
        mask_value = masks[r]
        bit_index = jnp.zeros((), jnp.int32)
        for k in range(1, low_bits + high_bits):
            bit_index = bit_index + (mask_value >= 1 << k).astype(jnp.int32)
        partner_txt = route(txt, bit_index, visit_dy, visit_dx, low_bits, high_bits)
        logits = tile_logits(img, partner_txt)
        g, loss = tile_weights(logits, zeros)
        image_grad = image_grad + left_product(g, partner_txt)
        outgoing = right_product(g, img)
        text_grad = text_grad + route(outgoing, bit_index, back_dy, back_dx, low_bits, high_bits)
        total_loss = total_loss + loss
    block_loss = (total_loss / (rows * rows * (ROUNDS + 1.0))).reshape(1)
    return (image_grad, text_grad, block_loss)


def solution(mesh):
    placed = (P(("dx", "dy"), None), P(("dx", "dy"), None), P(("dx", "dy"), None), P())
    return jax.shard_map(
        body,
        mesh=mesh,
        in_specs=placed,
        out_specs=(P(("dx", "dy"), None), P(("dx", "dy"), None), P(("dx", "dy"))),
        check_vma=False,
    )
```

profile of v0, /device:TPU:1, one launch (start us, length us, event | category | flops | bytes accessed | tf_op | source)
XLA Modules:
  0.0 154.3 jit_solution(3306009459217378720)
XLA Ops:
  0.6 0.0 copy-start
  0.6 1.4 fusion.13
  17.6 1.3 convert_element_type.228
  18.9 0.0 copy-done
  18.9 0.0 copy-start.1
  18.9 0.1 convert_element_type.229
  19.0 0.6 copy-done.1
  19.6 1.1 fusion.5
  20.7 10.5 %conditional.8 = (bf16[256,1152]{1,0:T(8,128)(2,1)}) conditional(s32[]{:T(128)} %bitcast.5, bf16[256,1152]{1,0:T(8,128)(2,1)S(1)} %convert_element_type.229, bf16[256,1152]{1,0:T(8,128)(2,1)S(1)} %convert_element_type.229, bf16[256,1152]{1,0:T(8,128)(2,1)S(1)} %convert_element_type.229, ...), branch_computations={%region_18.19_spmd, %region_19.20_spmd, %region_20.21_spmd, %regio... | conditional | bytes 2359344 | solution.py:81
  20.7 8.8 %collective-permute-start.18 = (bf16[256,1152]{1,0:T(8,128)(2,1)S(1)}, bf16[256,1152]{1,0:T(8,128)(2,1)}, u32[]{:S(2)}, u32[]{:S(2)}) collective-permute-start(bf16[256,1152]{1,0:T(8,128)(2,1)S(1)} %param.18), channel_id=1, source_target_pairs={{0,1},{1,0},{2,3},{3,2},{4,5},{5,4},{6,7},{7,6},{8,9},{9,8},{10,11... | collective-permute-start | bytes 1769480 | tf_op jit(solution)/shard_map/cond/branch_0_fun/ppermute | solution.py:29
  29.5 1.7 %collective-permute-done.18 = bf16[256,1152]{1,0:T(8,128)(2,1)} collective-permute-done((bf16[256,1152]{1,0:T(8,128)(2,1)S(1)}, bf16[256,1152]{1,0:T(8,128)(2,1)}, u32[]{:S(2)}, u32[]{:S(2)}) %collective-permute-start.18) | collective-permute-done | bytes 589856 | tf_op jit(solution)/shard_map/cond/branch_0_fun/ppermute | solution.py:29
  31.2 2.2 %fusion.8 = (f32[]{:T(128)}, f32[256,256]{1,0:T(8,128)S(1)}) fusion(bf16[256,1152]{1,0:T(8,128)(2,1)} %get-tuple-element.130, bf16[256,1152]{1,0:T(8,128)(2,1)S(1)} %convert_element_type.228), kind=kOutput, calls=%fused_computation.20 | convolution fusion | flops 151519232 | bytes 1441796 | tf_op jit(solution)/shard_map/dot_general | solution.py:34
  33.5 18.0 %conditional.7 = (bf16[256,1152]{1,0:T(8,128)(2,1)}) conditional(s32[]{:T(128)} %bitcast.3, bf16[256,1152]{1,0:T(8,128)(2,1)S(1)} %convert_element_type.229, bf16[256,1152]{1,0:T(8,128)(2,1)S(1)} %convert_element_type.229, bf16[256,1152]{1,0:T(8,128)(2,1)S(1)} %convert_element_type.229, ...), branch_computations={%region_9.10_spmd, %region_10.11_spmd, %region_11.12_spmd, %region... | conditional | bytes 2359344 | solution.py:81
  33.5 1.9 %collective-permute-start.17 = (bf16[256,1152]{1,0:T(8,128)(2,1)S(1)}, bf16[256,1152]{1,0:T(8,128)(2,1)}, u32[]{:S(2)}, u32[]{:S(2)}) collective-permute-start(bf16[256,1152]{1,0:T(8,128)(2,1)S(1)} %param.17), channel_id=1, source_target_pairs={{0,256},{256,0},{32,288},{288,32},{64,320},{320,64},{96,352},{352,... | collective-permute-start | bytes 1769480 | tf_op jit(solution)/shard_map/cond/branch_8_fun/ppermute | solution.py:29
  35.4 16.1 %collective-permute-done.17 = bf16[256,1152]{1,0:T(8,128)(2,1)} collective-permute-done((bf16[256,1152]{1,0:T(8,128)(2,1)S(1)}, bf16[256,1152]{1,0:T(8,128)(2,1)}, u32[]{:S(2)}, u32[]{:S(2)}) %collective-permute-start.17) | collective-permute-done | bytes 589856 | tf_op jit(solution)/shard_map/cond/branch_8_fun/ppermute | solution.py:29
  51.5 2.2 %fusion.7 = (f32[]{:T(128)}, f32[256,256]{1,0:T(8,128)S(1)}) fusion(bf16[256,1152]{1,0:T(8,128)(2,1)} %get-tuple-element.129, bf16[256,1152]{1,0:T(8,128)(2,1)S(1)} %convert_element_type.228), kind=kOutput, calls=%fused_computation.19 | convolution fusion | flops 151519232 | bytes 1441796 | tf_op jit(solution)/shard_map/dot_general | solution.py:34
  53.7 17.1 %conditional.6 = (bf16[256,1152]{1,0:T(8,128)(2,1)}) conditional(s32[]{:T(128)} %bitcast.1, bf16[256,1152]{1,0:T(8,128)(2,1)S(1)} %convert_element_type.229, bf16[256,1152]{1,0:T(8,128)(2,1)S(1)} %convert_element_type.229, bf16[256,1152]{1,0:T(8,128)(2,1)S(1)} %convert_element_type.229, ...), branch_computations={%region_0.1_spmd, %region_1.2_spmd, %region_2.3_spmd, %region_3.4_... | conditional | bytes 2359344 | solution.py:81
  53.7 1.9 %collective-permute-start.2 = (bf16[256,1152]{1,0:T(8,128)(2,1)S(1)}, bf16[256,1152]{1,0:T(8,128)(2,1)}, u32[]{:S(2)}, u32[]{:S(2)}) collective-permute-start(bf16[256,1152]{1,0:T(8,128)(2,1)S(1)} %param.2), channel_id=1, source_target_pairs={{0,4},{4,0},{1,5},{5,1},{2,6},{6,2},{3,7},{7,3},{8,12},{12,8},{9,1... | collective-permute-start | bytes 1769480 | tf_op jit(solution)/shard_map/cond/branch_2_fun/ppermute | solution.py:29
  55.6 15.2 %collective-permute-done.2 = bf16[256,1152]{1,0:T(8,128)(2,1)} collective-permute-done((bf16[256,1152]{1,0:T(8,128)(2,1)S(1)}, bf16[256,1152]{1,0:T(8,128)(2,1)}, u32[]{:S(2)}, u32[]{:S(2)}) %collective-permute-start.2) | collective-permute-done | bytes 589856 | tf_op jit(solution)/shard_map/cond/branch_2_fun/ppermute | solution.py:29
  70.8 2.2 %fusion.6 = (f32[]{:T(128)}, f32[256,256]{1,0:T(8,128)S(1)}) fusion(bf16[256,1152]{1,0:T(8,128)(2,1)} %get-tuple-element.128, bf16[256,1152]{1,0:T(8,128)(2,1)S(1)} %convert_element_type.228), kind=kOutput, calls=%fused_computation.18 | convolution fusion | flops 151519232 | bytes 1441796 | tf_op jit(solution)/shard_map/dot_general | solution.py:34
  75.6 0.4 fusion.12
  76.0 1.4 convolution_add_fusion.3
  77.4 1.4 convolution_add_fusion.2
  78.9 2.4 %convolution_add_fusion.1 = f32[256,1152]{1,0:T(8,128)} fusion(f32[256,1152]{1,0:T(8,128)S(1)} %convolution_add_fusion.2, bf16[256,1152]{1,0:T(8,128)(2,1)} %get-tuple-element.130, f32[256,256]{1,0:T(8,128)S(1)} %get-tuple-element.127), kind=kOutput, calls=%fused_computation.1 | convolution fusion | flops 151552000 | bytes 3211264 | tf_op jit(solution)/shard_map/dot_general | solution.py:48
  81.3 0.4 fusion.11
  81.7 6.7 %conditional.11 = (f32[256,1152]{1,0:T(8,128)}) conditional(s32[]{:T(128)} %bitcast.5, f32[256,1152]{1,0:T(8,128)S(1)} %fusion.11, f32[256,1152]{1,0:T(8,128)S(1)} %fusion.11, f32[256,1152]{1,0:T(8,128)S(1)} %fusion.11, f32[256,1152]{1,0:T(8,128)S(1)} %fusion.11, f32[256,1152]{1,0:T(8,128)S(1)} %fusion.11, ...), branch_computations={%region_45.46_spmd, %region_46.47_spmd, %region_47.48_spmd, %regio... | conditional | bytes 4718640 | solution.py:81
  81.7 4.0 %collective-permute-start.45 = (f32[256,1152]{1,0:T(8,128)S(1)}, f32[256,1152]{1,0:T(8,128)}, u32[]{:S(2)}, u32[]{:S(2)}) collective-permute-start(f32[256,1152]{1,0:T(8,128)S(1)} %param.45), channel_id=1, source_target_pairs={{0,1},{1,0},{2,3},{3,2},{4,5},{5,4},{6,7},{7,6},{8,9},{9,8},{10,11... | collective-permute-start | bytes 3538952 | tf_op jit(solution)/shard_map/cond/branch_0_fun/ppermute | solution.py:29
  85.8 2.6 %collective-permute-done.45 = f32[256,1152]{1,0:T(8,128)} collective-permute-done((f32[256,1152]{1,0:T(8,128)S(1)}, f32[256,1152]{1,0:T(8,128)}, u32[]{:S(2)}, u32[]{:S(2)}) %collective-permute-start.45) | collective-permute-done | bytes 1179680 | tf_op jit(solution)/shard_map/cond/branch_0_fun/ppermute | solution.py:29
  88.4 0.4 fusion.10
  88.8 30.7 %conditional.10 = (f32[256,1152]{1,0:T(8,128)}) conditional(s32[]{:T(128)} %bitcast.3, f32[256,1152]{1,0:T(8,128)S(1)} %fusion.10, f32[256,1152]{1,0:T(8,128)S(1)} %fusion.10, f32[256,1152]{1,0:T(8,128)S(1)} %fusion.10, f32[256,1152]{1,0:T(8,128)S(1)} %fusion.10, f32[256,1152]{1,0:T(8,128)S(1)} %fusion.10, ...), branch_computations={%region_36.37_spmd, %region_37.38_spmd, %region_38.39_spmd, %regio... | conditional | bytes 4718640 | solution.py:81
  88.8 2.2 %collective-permute-start.44 = (f32[256,1152]{1,0:T(8,128)S(1)}, f32[256,1152]{1,0:T(8,128)}, u32[]{:S(2)}, u32[]{:S(2)}) collective-permute-start(f32[256,1152]{1,0:T(8,128)S(1)} %param.44), channel_id=1, source_target_pairs={{0,256},{256,0},{32,288},{288,32},{64,320},{320,64},{96,352},{352,... | collective-permute-start | bytes 3538952 | tf_op jit(solution)/shard_map/cond/branch_8_fun/ppermute | solution.py:29
  91.1 28.4 %collective-permute-done.44 = f32[256,1152]{1,0:T(8,128)} collective-permute-done((f32[256,1152]{1,0:T(8,128)S(1)}, f32[256,1152]{1,0:T(8,128)}, u32[]{:S(2)}, u32[]{:S(2)}) %collective-permute-start.44) | collective-permute-done | bytes 1179680 | tf_op jit(solution)/shard_map/cond/branch_8_fun/ppermute | solution.py:29
  119.5 0.4 fusion.9
  119.9 29.8 %conditional.9 = (f32[256,1152]{1,0:T(8,128)}) conditional(s32[]{:T(128)} %bitcast.1, f32[256,1152]{1,0:T(8,128)S(1)} %fusion.9, f32[256,1152]{1,0:T(8,128)S(1)} %fusion.9, f32[256,1152]{1,0:T(8,128)S(1)} %fusion.9, f32[256,1152]{1,0:T(8,128)S(1)} %fusion.9, f32[256,1152]{1,0:T(8,128)S(1)} %fusion.9, ...), branch_computations={%region_27.28_spmd, %region_28.29_spmd, %region_29.30_spmd, %regio... | conditional | bytes 4718640 | solution.py:81
  119.9 1.9 %collective-permute-start.29 = (f32[256,1152]{1,0:T(8,128)S(1)}, f32[256,1152]{1,0:T(8,128)}, u32[]{:S(2)}, u32[]{:S(2)}) collective-permute-start(f32[256,1152]{1,0:T(8,128)S(1)} %param.29), channel_id=1, source_target_pairs={{0,4},{4,0},{1,5},{5,1},{2,6},{6,2},{3,7},{7,3},{8,12},{12,8},{9,1... | collective-permute-start | bytes 3538952 | tf_op jit(solution)/shard_map/cond/branch_2_fun/ppermute | solution.py:29
  121.9 27.8 %collective-permute-done.29 = f32[256,1152]{1,0:T(8,128)} collective-permute-done((f32[256,1152]{1,0:T(8,128)S(1)}, f32[256,1152]{1,0:T(8,128)}, u32[]{:S(2)}, u32[]{:S(2)}) %collective-permute-start.29) | collective-permute-done | bytes 1179680 | tf_op jit(solution)/shard_map/cond/branch_2_fun/ppermute | solution.py:29
  149.7 3.4 %fusion.1 = f32[256,1152]{1,0:T(8,128)} fusion(f32[256,1152]{1,0:T(8,128)} %get-tuple-element.133, f32[256,1152]{1,0:T(8,128)} %get-tuple-element.132, f32[256,1152]{1,0:T(8,128)} %get-tuple-element.131, bf16[256,1152]{1,0:T(8,128)(2,1)S(1)} %convert_element_type.228, f32[256,256]{1,0:T(8,128)S(1)} %get-tuple-element.121, s32[256]{0:T(256)S(1)} %bitcast.29), kind=kOutput, calls=%fused_computation.5 | convolution fusion | flops 152338432 | bytes 5571584 | tf_op jit(solution)/shard_map/dot_general | solution.py:52
Async XLA Ops:
  0.6 18.3 %copy-start = (f32[256,1152]{1,0:T(8,128)S(1)}, f32[256,1152]{1,0:T(8,128)}, u32[]{:S(2)}) copy-start(f32[256,1152]{1,0:T(8,128)} %param.59) | copy-start | bytes 3538948
  18.9 0.7 copy-start.1
  20.7 10.5 %collective-permute-start.18 = (bf16[256,1152]{1,0:T(8,128)(2,1)S(1)}, bf16[256,1152]{1,0:T(8,128)(2,1)}, u32[]{:S(2)}, u32[]{:S(2)}) collective-permute-start(bf16[256,1152]{1,0:T(8,128)(2,1)S(1)} %param.18), channel_id=1, source_target_pairs={{0,1},{1,0},{2,3},{3,2},{4,5},{5,4},{6,7},{7,6},{8,9},{9,8},{10,11... | collective-permute-start | bytes 1769480 | tf_op jit(solution)/shard_map/cond/branch_0_fun/ppermute | solution.py:29
  33.5 18.0 %collective-permute-start.17 = (bf16[256,1152]{1,0:T(8,128)(2,1)S(1)}, bf16[256,1152]{1,0:T(8,128)(2,1)}, u32[]{:S(2)}, u32[]{:S(2)}) collective-permute-start(bf16[256,1152]{1,0:T(8,128)(2,1)S(1)} %param.17), channel_id=1, source_target_pairs={{0,256},{256,0},{32,288},{288,32},{64,320},{320,64},{96,352},{352,... | collective-permute-start | bytes 1769480 | tf_op jit(solution)/shard_map/cond/branch_8_fun/ppermute | solution.py:29
  53.7 17.1 %collective-permute-start.2 = (bf16[256,1152]{1,0:T(8,128)(2,1)S(1)}, bf16[256,1152]{1,0:T(8,128)(2,1)}, u32[]{:S(2)}, u32[]{:S(2)}) collective-permute-start(bf16[256,1152]{1,0:T(8,128)(2,1)S(1)} %param.2), channel_id=1, source_target_pairs={{0,4},{4,0},{1,5},{5,1},{2,6},{6,2},{3,7},{7,3},{8,12},{12,8},{9,1... | collective-permute-start | bytes 1769480 | tf_op jit(solution)/shard_map/cond/branch_2_fun/ppermute | solution.py:29
  81.7 6.6 %collective-permute-start.45 = (f32[256,1152]{1,0:T(8,128)S(1)}, f32[256,1152]{1,0:T(8,128)}, u32[]{:S(2)}, u32[]{:S(2)}) collective-permute-start(f32[256,1152]{1,0:T(8,128)S(1)} %param.45), channel_id=1, source_target_pairs={{0,1},{1,0},{2,3},{3,2},{4,5},{5,4},{6,7},{7,6},{8,9},{9,8},{10,11... | collective-permute-start | bytes 3538952 | tf_op jit(solution)/shard_map/cond/branch_0_fun/ppermute | solution.py:29
  88.8 30.7 %collective-permute-start.44 = (f32[256,1152]{1,0:T(8,128)S(1)}, f32[256,1152]{1,0:T(8,128)}, u32[]{:S(2)}, u32[]{:S(2)}) collective-permute-start(f32[256,1152]{1,0:T(8,128)S(1)} %param.44), channel_id=1, source_target_pairs={{0,256},{256,0},{32,288},{288,32},{64,320},{320,64},{96,352},{352,... | collective-permute-start | bytes 3538952 | tf_op jit(solution)/shard_map/cond/branch_8_fun/ppermute | solution.py:29
  119.9 29.8 %collective-permute-start.29 = (f32[256,1152]{1,0:T(8,128)S(1)}, f32[256,1152]{1,0:T(8,128)}, u32[]{:S(2)}, u32[]{:S(2)}) collective-permute-start(f32[256,1152]{1,0:T(8,128)S(1)} %param.29), channel_id=1, source_target_pairs={{0,4},{4,0},{1,5},{5,1},{2,6},{6,2},{3,7},{7,3},{8,12},{12,8},{9,1... | collective-permute-start | bytes 3538952 | tf_op jit(solution)/shard_map/cond/branch_2_fun/ppermute | solution.py:29
where the time goes:
time: 155 us; the launch traced here: 154 us
  waiting for transfers between devices  91.9 us (59%)
  starting transfers between devices  20.8 us (13%)
  between operations  20 us (13%)
  matrix products  18.1 us (12%)
  local copies, waits for them, and re-layouts  1.98 us (1%)
    ppermute x6, waiting for transfers between devices, from_partner(): return lax.ppermute(block, axis, route)  91.9 us
    ppermute x6, starting transfers between devices, from_partner(): return lax.ppermute(block, axis, route)  20.8 us
    dot_general x4, matrix products, tile_logits(): lax.dot_general(img_block, txt_block, (((1,), (1,)), ((), ())), preferred...  7.75 us
    dot_general x4, matrix products, left_product(): return jnp.dot(g, txt_block, preferred_element_type=jnp.float32)  5.7 us
    dot_general x4, matrix products, right_product(): lax.dot_general(g, img_block, (((0,), (0,)), ((), ())), preferred_element...  4.66 us
  transfers between devices with their start and end apart: 6, of which 6 were waited for; matrix products, arithmetic and copies ran while one was open for 0% of the time, Pallas kernels for 0%

commit v1 on v0

v1 whole, which is shorter than its diff:
```python
from functools import partial

import jax
import jax.numpy as jnp
from jax import lax
from jax.experimental import pallas as pl
from jax.experimental.pallas import tpu as pltpu
from jax.sharding import PartitionSpec as P

MESH = pl.DeviceIdType.MESH
BIAS = -2.0
CHUNK = 32

SECOND = 8
FAR = {8: (7,), 2: (1,), 4: (3, 6, 5)}


def plan_for(bits):
    place_of = {bit: ("recv", slot) for slot, bit in enumerate(bits)}
    relays = 0
    streams = []
    forwards = []
    for bit in (4, 8, 2):
        if bit not in bits:
            continue
        near = next((b for b in FAR[bit] if b in bits), None)
        if near is None:
            near = FAR[bit][-1]
            place_of[near] = ("relay", relays)
            relays += 1
        forwards.append((near, bit))
    for near, _ in forwards:
        streams.append((1 << near, place_of[near]))
    forwarded = {near for near, _ in forwards}
    reached = {far for _, far in forwards}
    for bit in bits:
        if bit not in forwarded and bit not in reached:
            streams.append((1 << bit, place_of[bit]))
    hops = [
        (streams.index((1 << near, place_of[near])), 1 << near | 1 << far, place_of[far])
        for near, far in forwards
    ]
    return streams, hops, relays


def exchange(streams, hops, low_count, images_ref, texts_ref, recv, own, relay, send_sem, recv_sem):
    dx, dy = lax.axis_index("dx"), lax.axis_index("dy")

    def flipped(index, mask):
        for k in range(16):
            if mask >> k & 1:
                step = 1 << k
                index = index + step * (1 - 2 * ((index // step) % 2))
        return index

    def device(mask):
        return (flipped(dx, mask // low_count), flipped(dy, mask % low_count))

    targets = [mask for mask, _ in streams] + [mask for _, mask, _ in hops]
    barrier = pltpu.get_barrier_semaphore()
    for mask in targets:
        pl.semaphore_signal(barrier, inc=1, device_id=device(mask), device_id_type=MESH)
    half = texts_ref.shape[0]
    own[pl.ds(0, half), :] = texts_ref[...].astype(jnp.bfloat16)
    own[pl.ds(half, half), :] = images_ref[...].astype(jnp.bfloat16)
    pl.semaphore_wait(barrier, len(targets))

    buffers = {"recv": recv, "relay": relay}

    def ref_of(place):
        return buffers[place[0]].at[place[1]]

    def copy(index, source, place, mask, chunk):
        rows = pl.ds(pl.multiple_of(chunk * CHUNK, CHUNK), CHUNK)
        return pltpu.make_async_remote_copy(
            src_ref=source.at[rows],
            dst_ref=ref_of(place).at[rows],
            send_sem=send_sem.at[index, chunk],
            recv_sem=recv_sem.at[index, chunk],
            device_id=device(mask),
            device_id_type=MESH,
        )

    def first(index, chunk):
        mask, place = streams[index]
        return copy(index, own, place, mask, chunk)

    def second(index, chunk):
        via, mask, place = hops[index]
        return copy(len(streams) + index, ref_of(streams[via][1]), place, mask, chunk)

    chunks = 2 * half // CHUNK

    @pl.loop(0, chunks)
    def _(chunk):
        for index in range(len(streams)):
            first(index, chunk).start()

    @pl.loop(0, chunks)
    def _(chunk):
        for index in range(len(hops)):
            first(hops[index][0], chunk).wait_recv()
            second(index, chunk).start()

    vias = {via for via, _, _ in hops}

    @pl.loop(0, chunks)
    def _(chunk):
        for index in range(len(streams)):
            first(index, chunk).wait_send()
            if index not in vias:
                first(index, chunk).wait_recv()
        for index in range(len(hops)):
            second(index, chunk).wait()


def exchange_call(bits, number, low_count, images, texts):
    half, width = images.shape
    streams, hops, relays = plan_for(bits)
    chunks = 2 * half // CHUNK
    total = len(streams) + len(hops)
    return pl.pallas_call(
        partial(exchange, streams, hops, low_count),
        out_shape=jax.ShapeDtypeStruct((len(bits), 2 * half, width), jnp.bfloat16),
        in_specs=[pl.BlockSpec(memory_space=pltpu.VMEM)] * 2,
        out_specs=pl.BlockSpec(memory_space=pl.ANY),
        scratch_shapes=[
            pltpu.VMEM((2 * half, width), jnp.bfloat16),
            pltpu.VMEM((max(relays, 1), 2 * half, width), jnp.bfloat16),
            pltpu.SemaphoreType.DMA((total, chunks)),
            pltpu.SemaphoreType.DMA((total, chunks)),
        ],
        compiler_params=pltpu.CompilerParams(
            collective_id=number, has_side_effects=True, vmem_limit_bytes=32 * 2**20
        ),
        name="exchange_" + "_".join(str(bit) for bit in bits),
    )(images, texts)


def across(a, b):
    return lax.dot_general(a, b, (((1,), (1,)), ((), ())), preferred_element_type=jnp.float32)


def sigmoid_parts(logits):
    e = jnp.exp(-jnp.abs(logits))
    return jnp.where(logits >= 0, 1.0, e) / (1.0 + e), e


def tiles(scale, images_ref, texts_ref, match_ref, recv, image_grad, text_grad, loss_ref, own):
    step = pl.program_id(0)
    half = texts_ref.shape[0]

    @pl.when(step == 0)
    def _():
        txt = texts_ref[...].astype(jnp.bfloat16)
        img = images_ref[...].astype(jnp.bfloat16)
        own[0] = txt
        own[1] = img
        logits = across(txt, img) + BIAS
        row = lax.broadcasted_iota(jnp.int32, logits.shape, 0)
        hit = row == match_ref[...]
        s, e = sigmoid_parts(logits)
        g = (s - jnp.where(hit, 1.0, 0.0)).astype(jnp.bfloat16)
        loss = jnp.maximum(jnp.where(hit, -logits, logits), 0.0) + jnp.log1p(e)
        loss_ref[0] = jnp.sum(loss) * scale
        text_grad[...] = jnp.dot(g, img, preferred_element_type=jnp.float32)
        image_grad[...] = lax.dot_general(
            g, txt, (((0,), (0,)), ((), ())), preferred_element_type=jnp.float32
        )

    @pl.when(step > 0)
    def _():
        other_txt = recv[0, pl.ds(0, half), :]
        logits = across(own[1], other_txt) + BIAS
        s, e = sigmoid_parts(logits)
        loss_ref[0] += jnp.sum(jnp.maximum(logits, 0.0) + jnp.log1p(e)) * scale
        image_grad[...] += jnp.dot(
            s.astype(jnp.bfloat16), other_txt, preferred_element_type=jnp.float32
        )
        other_img = recv[0, pl.ds(half, half), :]
        s, _ = sigmoid_parts(across(own[0], other_img) + BIAS)
        text_grad[...] += jnp.dot(
            s.astype(jnp.bfloat16), other_img, preferred_element_type=jnp.float32
        )


def tiles_call(images, texts, match, recv):
    half, width = images.shape
    rounds = recv.shape[0]
    whole = pl.BlockSpec((half, width), lambda i: (0, 0))
    grad = jax.ShapeDtypeStruct((half, width), jnp.float32)
    flops = 2 * half * half * width * (3 + 4 * rounds)
    return pl.pallas_call(
        partial(tiles, 1.0 / (half * half * (rounds + 1.0))),
        grid=(rounds + 1,),
        out_shape=(grad, grad, jax.ShapeDtypeStruct((1,), jnp.float32)),
        in_specs=[
            whole,
            whole,
            pl.BlockSpec((1, half), lambda i: (0, 0)),
            pl.BlockSpec((1, 2 * half, width), lambda i: (jnp.maximum(i - 1, 0), 0, 0)),
        ],
        out_specs=(whole, whole, pl.BlockSpec(memory_space=pltpu.SMEM)),
        scratch_shapes=[pltpu.VMEM((2, half, width), jnp.bfloat16)],
        compiler_params=pltpu.CompilerParams(vmem_limit_bytes=40 * 2**20),
        cost_estimate=pl.CostEstimate(
            flops=flops, bytes_accessed=16 * half * width + recv.size * 2, transcendentals=0
        ),
        name="tiles",
    )(images, texts, match, recv)


def body(low_count, all_bits, images, texts, match, masks):
    low_bits = low_count.bit_length() - 1
    sets, number = [], {}
    table = []
    for one in range(all_bits):
        for other in range(all_bits):
            low, high = min(one, other), max(one, other)
            if low == high or low >= low_bits or SECOND in (low, high):
                table.append(0)
                continue
            if (low, high) not in number:
                number[low, high] = len(sets)
                sets.append((low, high, SECOND))
            table.append(number[low, high])
    bit = jnp.sum((masks[:, None] >= (1 << jnp.arange(1, all_bits))[None, :]).astype(jnp.int32), 1)
    index = jnp.array(table, jnp.int32)[bit[0] * all_bits + bit[2]]
    branches = [
        partial(exchange_call, bits, at, low_count) for at, bits in enumerate(sets)
    ]
    recv = lax.switch(index, branches, images, texts)
    return tiles_call(images, texts, match, recv)


def solution(mesh):
    rows = P(("dx", "dy"), None)
    low_count = mesh.shape["dy"]
    all_bits = (low_count * mesh.shape["dx"]).bit_length() - 1
    return jax.shard_map(
        partial(body, low_count, all_bits),
        mesh=mesh,
        in_specs=(rows, rows, rows, P()),
        out_specs=(rows, rows, P(("dx", "dy"))),
        check_vma=False,
    )
```

time: 155 us -> 54.2 us (0.35)
  the two profiles are of different devices: /device:TPU:1 before, /device:TPU:16 now
where the time goes in v1:
time: 54.2 us; the launch traced here: 54 us
  Pallas kernels  48.6 us (90%)
  between operations  2.62 us (5%)
  local copies, waits for them, and re-layouts  1.84 us (3%)
  other arithmetic  0.84 us (2%)
    pallas_call x1, Pallas kernels, exchange_call(): pl.pallas_call(partial(exchange, streams, hops, low_count), out_shape=jax...  38.7 us
    pallas_call x1, Pallas kernels, tiles_call(): pl.pallas_call(partial(tiles, 1.0 / (half * half * (rounds + 1.0))), grid...  9.88 us
    dynamic_slice x1, local copies, waits for them, and re-layouts, body(): index = jnp.array(table, jnp.int32)[bit[0] * all_bits + bit[2]]  1.24 us

profile of v1, /device:TPU:16, one launch (start us, length us, event | category | flops | bytes accessed | tf_op | source)
XLA Modules:
  0.0 54.0 jit_solution(15227934352456967089)
XLA Ops:
  0.6 0.8 %convert_reduce_fusion = s32[3]{0:T(128)S(1)} fusion(s32[8]{0:T(128)S(1)} %add_shift-left_fusion, s32[3]{0:T(128)} %param.33), kind=kLoop, calls=%fused_computation | loop fusion | flops 69 | bytes 56 | tf_op jit(solution)/shard_map/reduce_sum | solution.py:227
  1.5 0.6 %fusion = (s32[1]{0:T(128)}, s32[1]{0:T(128)}) fusion(s32[3]{0:T(128)S(1)} %convert_reduce_fusion), kind=kLoop, calls=%fused_computation.2 | loop fusion | bytes 16 | tf_op jit(solution)/shard_map/slice | solution.py:228
  3.4 1.2 %dynamic_slice.3 = s32[1]{0:T(128)} dynamic-slice(s32[81]{0:T(128)} %constant.16.clone, s32[]{:T(128)S(6)} %select_n.3), dynamic_slice_sizes={1} | dynamic-slice | bytes 12 | tf_op jit(solution)/shard_map/dynamic_slice | solution.py:228
  5.3 0.0 copy-start
  5.3 38.8 %conditional.1 = (bf16[3,512,1152]{2,1,0:T(8,128)(2,1)S(1)}) conditional(s32[]{:T(128)} %bitcast.1, (f32[256,1152]{1,0:T(8,128)}, f32[256,1152]{1,0:T(8,128)}) %tuple.82, (f32[256,1152]{1,0:T(8,128)}, f32[256,1152]{1,0:T(8,128)}) %tuple.82, (f32[256,1152]{1,0:T(8,128)}, f32[256,1152]{1,0:T(8,128)}) %tuple.82, ...), branch_computations={%region_1.0_spmd, %region_2.0_spmd, %region_3.0_spmd, %region_4.0_... | conditional | bytes 8 | solution.py:232
  5.3 38.7 %exchange_0_7_8.1 = bf16[3,512,1152]{2,1,0:T(8,128)(2,1)S(1)} custom-call(f32[256,1152]{1,0:T(8,128)} %get-tuple-element.126.images_ref, f32[256,1152]{1,0:T(8,128)} %get-tuple-element.127.texts_ref), custom_call_target="tpu_custom_call" | custom-call | tf_op jit(solution)/shard_map/cond/branch_6_fun/exchange_0_7_8/pallas_call | solution.py:122
  44.1 0.0 copy-done
  44.1 9.9 %tiles.1 = (f32[256,1152]{1,0:T(8,128)}, f32[256,1152]{1,0:T(8,128)}, f32[1]{0:T(128)}) custom-call(f32[256,1152]{1,0:T(8,128)} %images_ref.1, f32[256,1152]{1,0:T(8,128)} %texts_ref.1, s32[1,256]{1,0:T(1,128)S(1)} %copy-done, bf16[3,512,1152]{2,1,0:T(8,128)(2,1)S(1)} %get-tuple-element.181.recv), custom_call_target="tpu_custom_call" | custom-call | flops 2264924160 | bytes 8257536 | tf_op jit(solution)/shard_map/tiles/pallas_call | solution.py:193
  (1 shorter events, 0.0 us)
Async XLA Ops:
  5.3 38.8 %copy-start = (s32[1,256]{1,0:T(1,128)S(1)}, s32[1,256]{1,0:T(1,128)}, u32[]{:S(2)}) copy-start(s32[1,256]{1,0:T(1,128)} %match_ref.1) | copy-start | bytes 3076

commit v2 on v0

v2 whole, which is shorter than its diff:
```python
from functools import partial

import jax
import jax.numpy as jnp
from jax import lax
from jax.experimental import pallas as pl
from jax.experimental.pallas import tpu as pltpu
from jax.sharding import PartitionSpec as P

MESH = pl.DeviceIdType.MESH
BIAS = -2.0
SECOND = 8
WIDE = 384
ROWS = 64
PIECE = 32

LOAD = {0: 0.2, 1: 1, 2: 1.01, 3: 4, 4: 4.01, 5: 1, 6: 2, 7: 1, 8: 1.02}
RELAYED = {(1, 2), (3, 4), (4, 5), (4, 6), (7, 8)}


def plan_for(bits):
    order = sorted(bits, key=lambda bit: LOAD[bit])
    for pair in RELAYED:
        if set(pair) <= set(bits) and LOAD[order[-1]] < 2 * max(LOAD[bit] for bit in pair):
            near, far = sorted(pair, key=lambda bit: LOAD[bit])
            (other,) = set(bits) - set(pair)
            return near, far, [(bit, half) for bit in (near, other, far) for half in (0, 1)]
    light = [bit for bit in order if LOAD[bit] * 3 <= LOAD[order[-1]]]
    heavy = [bit for bit in order if bit not in light]
    places = [(bit, half) for bit in light for half in (0, 1)]
    return None, None, places + [(bit, half) for half in (0, 1) for bit in heavy]


def flipped(index, mask):
    for k in range(16):
        if mask >> k & 1:
            step = 1 << k
            index = index + step * (1 - 2 * ((index // step) % 2))
    return index


def meet(bits, scale, low_count, *refs):
    (images_ref, texts_ref, match_ref, image_ref, text_ref, loss_ref, *refs) = refs
    (wide, blocks, grads, labels, logits, g, losses, *refs) = refs
    (load_sem, send_sem, recv_sem, near_sem, store_sem) = refs
    near, far, places = plan_for(bits)
    half_rows, width = texts_ref.shape
    pieces = half_rows // PIECE
    dx, dy = lax.axis_index("dx"), lax.axis_index("dy")

    def device(mask):
        return (flipped(dx, mask // low_count), flipped(dy, mask % low_count))

    at = {place: 2 + k for k, place in enumerate(places)}
    masks = {bit: 1 << bit for bit in bits}
    if far is not None:
        masks[far] = 1 << near | 1 << far

    def half_copy(bit, half):
        return pltpu.make_async_remote_copy(
            src_ref=blocks.at[half],
            dst_ref=blocks.at[at[bit, half]],
            send_sem=send_sem.at[at[bit, half]],
            recv_sem=recv_sem.at[at[bit, half]],
            device_id=device(masks[bit]),
            device_id_type=MESH,
        )

    def piece_copy(half, piece, forward):
        rows = pl.ds(pl.multiple_of(piece * PIECE, PIECE), PIECE)
        here, there = (at[near, 0] + half, at[far, 0] + half) if forward else (half, at[near, 0] + half)
        return pltpu.make_async_remote_copy(
            src_ref=blocks.at[here, rows],
            dst_ref=blocks.at[there, rows],
            send_sem=send_sem.at[there],
            recv_sem=recv_sem.at[there] if forward else near_sem.at[half, piece],
            device_id=device(masks[far if forward else near]),
            device_id_type=MESH,
        )

    loads = [
        pltpu.make_async_copy(ref, wide.at[half], load_sem.at[half])
        for half, ref in enumerate((texts_ref, images_ref))
    ]
    for load in loads:
        load.start()
    barrier = pltpu.get_barrier_semaphore()
    for bit in bits:
        pl.semaphore_signal(barrier, inc=1, device_id=device(masks[bit]), device_id_type=MESH)
    for half in (0, 1):
        loads[half].wait()

        @pl.loop(0, half_rows // ROWS)
        def _(step, half=half):
            rows = pl.ds(pl.multiple_of(step * ROWS, ROWS), ROWS)
            blocks[half, rows, :] = wide[half, rows, :].astype(jnp.bfloat16)

        if half == 0:
            pl.semaphore_wait(barrier, len(bits))
        if near is not None:

            @pl.loop(0, pieces)
            def _(piece, half=half):
                piece_copy(half, piece, False).start()

        for bit in sorted(bits, key=lambda bit: -LOAD[bit]):
            if bit not in (near, far):
                half_copy(bit, half).start()

    @pl.loop(0, half_rows // ROWS)
    def _(step):
        rows = pl.ds(pl.multiple_of(step * ROWS, ROWS), ROWS)
        zero = jnp.zeros((ROWS, width), jnp.float32)
        grads[0, rows, :] = zero
        grads[1, rows, :] = zero

    square = (half_rows, half_rows)
    row = lax.broadcasted_iota(jnp.int32, square, 0)
    column = lax.broadcasted_iota(jnp.int32, square, 1)
    short = jnp.bfloat16
    hits = jnp.where(row == match_ref[...], 1.0, 0.0).astype(short)
    labels[1] = hits
    labels[0] = across(jnp.where(row == column, 1.0, 0.0).astype(short), hits).astype(short)
    labels[2] = jnp.zeros(square, short)
    losses[...] = jnp.zeros_like(losses)

    ready = 2 if near is None else 4
    last_text = max(k for (_, half), k in at.items() if half == 0)
    store_image = pltpu.make_async_copy(grads.at[0], image_ref, store_sem.at[0])
    store_text = pltpu.make_async_copy(grads.at[1], text_ref, store_sem.at[1])

    @pl.loop(0, 2 + len(places))
    def _(k):
        side = (k == 1).astype(jnp.int32)
        for (_, half), place in at.items():
            if half == 1:
                side += (k == place).astype(jnp.int32)

        if near is not None:

            @pl.when(k == 2)
            def _():
                for half in (0, 1):

                    @pl.loop(0, pieces)
                    def _(piece, half=half):
                        piece_copy(half, piece, False).wait_recv()
                        piece_copy(half, piece, True).start()

        @pl.when(k >= ready)
        def _():
            pltpu.make_async_copy(blocks.at[k], blocks.at[k], recv_sem.at[k]).wait()

        logits[...] = jnp.full(square, BIAS, jnp.float32)

        @pl.loop(0, width // WIDE)
        def _(step):
            columns = pl.ds(pl.multiple_of(step * WIDE, WIDE), WIDE)
            logits[...] += across(blocks[1 - side, :, columns], blocks[k, :, columns])

        @pl.loop(0, half_rows // ROWS)
        def _(step):
            rows = pl.ds(pl.multiple_of(step * ROWS, ROWS), ROWS)
            x = logits[rows, :]
            label = labels[jnp.minimum(k, 2), rows, :].astype(jnp.float32)
            e = jnp.exp(-jnp.abs(x))
            s = jnp.where(x >= 0, 1.0, e) / (1.0 + e)
            g[rows, :] = (s - label).astype(short)
            loss = jnp.maximum(jnp.where(label > 0, -x, x), 0.0) + jnp.log1p(e)
            loss = jnp.sum(loss.reshape(ROWS // 8, 8, half_rows), axis=0)
            losses[...] += jnp.where(side == 0, loss, 0.0)

        @pl.loop(0, width // WIDE)
        def _(step):
            columns = pl.ds(pl.multiple_of(step * WIDE, WIDE), WIDE)
            grads[side, :, columns] += times(g[...], blocks[k, :, columns])

        @pl.when(k == last_text)
        def _():
            store_image.start()

    store_text.start()
    loss_ref[0] = jnp.sum(losses[...]) * scale
    for bit in bits:
        for half in (0, 1):
            half_copy(bit, half).wait_send()
    store_image.wait()
    store_text.wait()


def meet_call(bits, number, scale, low_count, images, texts, match):
    half, width = images.shape
    places = 2 + 2 * len(bits)
    grad = jax.ShapeDtypeStruct((half, width), jnp.float32)
    vmem = pl.BlockSpec(memory_space=pltpu.VMEM)
    anywhere = pl.BlockSpec(memory_space=pl.ANY)
    return pl.pallas_call(
        partial(meet, bits, scale, low_count),
        out_shape=(grad, grad, jax.ShapeDtypeStruct((1,), jnp.float32)),
        in_specs=[anywhere, anywhere, vmem],
        out_specs=(anywhere, anywhere, pl.BlockSpec(memory_space=pltpu.SMEM)),
        scratch_shapes=[
            pltpu.VMEM((2, half, width), jnp.float32),
            pltpu.VMEM((places, half, width), jnp.bfloat16),
            pltpu.VMEM((2, half, width), jnp.float32),
            pltpu.VMEM((3, half, half), jnp.bfloat16),
            pltpu.VMEM((half, half), jnp.float32),
            pltpu.VMEM((half, half), jnp.bfloat16),
            pltpu.VMEM((8, half), jnp.float32),
            pltpu.SemaphoreType.DMA((2,)),
            pltpu.SemaphoreType.DMA((places,)),
            pltpu.SemaphoreType.DMA((places,)),
            pltpu.SemaphoreType.DMA((2, half // PIECE)),
            pltpu.SemaphoreType.DMA((2,)),
        ],
        compiler_params=pltpu.CompilerParams(
            collective_id=number, has_side_effects=True, vmem_limit_bytes=24 * 2**20
        ),
        cost_estimate=pl.CostEstimate(
            flops=32 * half * half * width, bytes_accessed=16 * half * width, transcendentals=0
        ),
        name="meet_" + "_".join(str(bit) for bit in bits),
    )(images, texts, match)


def across(a, b):
    return lax.dot_general(a, b, (((1,), (1,)), ((), ())), preferred_element_type=jnp.float32)


def times(a, b):
    return jnp.dot(a, b, preferred_element_type=jnp.float32)


def choose(all_bits, masks_ref, index_ref):
    first, third = masks_ref[0], masks_ref[2]
    low, high = jnp.minimum(first, third), jnp.maximum(first, third)
    low_bit, high_bit = jnp.int32(0), jnp.int32(0)
    for k in range(1, all_bits):
        low_bit += (low >= 1 << k).astype(jnp.int32)
        high_bit += (high >= 1 << k).astype(jnp.int32)
    before = low_bit * (all_bits - 1) - low_bit * (low_bit + 1) // 2
    index_ref[0] = before + high_bit - low_bit - 1


def body(low_count, all_bits, images, texts, match, masks):
    low_bits = low_count.bit_length() - 1
    half = images.shape[0]
    scale = 1.0 / (half * half * (masks.shape[0] + 1.0))
    smem = pl.BlockSpec(memory_space=pltpu.SMEM)
    index = pl.pallas_call(
        partial(choose, all_bits),
        out_shape=jax.ShapeDtypeStruct((1,), jnp.int32),
        in_specs=[smem],
        out_specs=smem,
        name="choose",
    )(masks)
    sets = [
        (low, high, SECOND) for low in range(low_bits) for high in range(low + 1, all_bits - 1)
    ]
    branches = [
        partial(meet_call, bits, number, scale, low_count) for number, bits in enumerate(sets)
    ]
    return lax.switch(index[0], branches, images, texts, match)


def solution(mesh):
    rows = P(("dx", "dy"), None)
    low_count = mesh.shape["dy"]
    all_bits = (low_count * mesh.shape["dx"]).bit_length() - 1
    return jax.shard_map(
        partial(body, low_count, all_bits),
        mesh=mesh,
        in_specs=(rows, rows, rows, P()),
        out_specs=(rows, rows, P(("dx", "dy"))),
        check_vma=False,
    )
```

time: 155 us -> 45.4 us (0.29)
  the two profiles are of different devices: /device:TPU:1 before, /device:TPU:4 now
where the time goes in v2:
time: 45.4 us; the launch traced here: 45.2 us
  Pallas kernels  39.8 us (88%)
  between operations  3.06 us (7%)
  local copies, waits for them, and re-layouts  2.03 us (4%)
    pallas_call x1, Pallas kernels, meet_call(): pl.pallas_call(partial(meet, bits, scale, low_count), out_shape=(grad, gr...  38.5 us
    unnamed x2, local copies, waits for them, and re-layouts  2.03 us
    pallas_call x1, Pallas kernels, body(): pl.pallas_call(partial(choose, all_bits), out_shape=jax.ShapeDtypeStruct(...  1.21 us

profile of v2, /device:TPU:4, one launch (start us, length us, event | category | flops | bytes accessed | tf_op | source)
XLA Modules:
  0.0 45.2 jit_solution(3589039776234891221)
XLA Ops:
  0.6 1.2 %choose.1 = s32[1]{0:T(128)} custom-call(s32[3]{0:T(128)} %masks_ref.1), custom_call_target="tpu_custom_call" | custom-call | tf_op jit(solution)/shard_map/choose/pallas_call | solution.py:250
  2.5 38.9 %conditional.1 = ((f32[256,1152]{1,0:T(8,128)S(1)}, f32[256,1152]{1,0:T(8,128)S(1)}, f32[1]{0:T(128)})) conditional(s32[]{:T(128)} %bitcast, (f32[256,1152]{1,0:T(8,128)}, f32[256,1152]{1,0:T(8,128)}, s32[1,256]{1,0:T(1,128)}) %tuple.82, (f32[256,1152]{1,0:T(8,128)}, f32[256,1152]{1,0:T(8,128)}, ...), branch_computations={%region_0.0_spmd, %region_1.0_spmd, %region_2.0_spmd, %region_3.0_... | conditional | flops 2415919104 | bytes 4718600 | solution.py:263
  2.5 38.5 %meet_0_2_8.1 = (f32[256,1152]{1,0:T(8,128)S(1)}, f32[256,1152]{1,0:T(8,128)S(1)}, f32[1]{0:T(128)}) custom-call(f32[256,1152]{1,0:T(8,128)} %get-tuple-element.153.refs_0_, f32[256,1152]{1,0:T(8,128)} %get-tuple-element.154.refs_1_, s32[1,256]{1,0:T(1,128)} %get-tuple-element.155.refs_2_), custom_call_target="tpu_custom_call" | custom-call | flops 2415919104 | bytes 4718592 | tf_op jit(solution)/shard_map/cond/branch_1_fun/meet_0_2_8/pallas_call | solution.py:197
  41.4 1.0 %copy.160 = f32[256,1152]{1,0:T(8,128)} copy(f32[256,1152]{1,0:T(8,128)S(1)} %get-tuple-element.384) | data formatting | bytes 2359296
  42.4 1.0 %copy.161 = f32[256,1152]{1,0:T(8,128)} copy(f32[256,1152]{1,0:T(8,128)S(1)} %get-tuple-element.385) | data formatting | bytes 2359296

commit v3 on v2

v3 whole, which is shorter than its diff:
```python
from functools import partial

import jax
import jax.numpy as jnp
from jax import lax
from jax.experimental import pallas as pl
from jax.experimental.pallas import tpu as pltpu
from jax.sharding import PartitionSpec as P

MESH = pl.DeviceIdType.MESH
BIAS = -2.0
SECOND = 8
WIDE = 384
ROWS = 64
PIECE = 32

LOAD = {0: 0.2, 1: 1, 2: 1.01, 3: 4, 4: 4.01, 5: 1, 6: 2, 7: 1, 8: 1.02}
RELAYED = {(1, 2), (3, 4), (4, 5), (4, 6), (7, 8)}


def plan_for(bits, half_rows):
    def whole(bit, half):
        return half, [(bit, 0, 0, half_rows)]

    order = sorted(bits, key=lambda bit: LOAD[bit])
    for pair in RELAYED:
        if set(pair) <= set(bits) and LOAD[order[-1]] < 2 * max(LOAD[bit] for bit in pair):
            near, far = sorted(pair, key=lambda bit: LOAD[bit])
            (other,) = set(bits) - set(pair)
            pieces = half_rows // PIECE
            if LOAD[other] * 2 < LOAD[far]:
                uses = [(other, 0), (other, 1), (near, 0), (far, 0), (near, 1), (far, 1)]
                passed = [0, 0, pieces // 4, pieces // 2, pieces, pieces * 3 // 2, 2 * pieces, 2 * pieces]
            else:
                uses = [(near, 0), (other, 0), (far, 0), (near, 1), (other, 1), (far, 1)]
                passed = [0, 0, pieces, pieces * 5 // 4, pieces * 3 // 2, 2 * pieces, 2 * pieces, 2 * pieces]
            return near, far, [whole(*use) for use in uses], passed
    light = [bit for bit in order if LOAD[bit] * 3 <= LOAD[order[-1]]]
    heavy = [bit for bit in order if bit not in light]
    tiles = [whole(bit, half) for bit in light for half in (0, 1)] + [whole(bit, 0) for bit in heavy]
    sent = dict.fromkeys(heavy, 0)
    for at in range(len(heavy)):
        parts, filled = [], 0
        for turn, bit in enumerate(heavy):
            rows = half_rows // len(heavy) // 16 * 16
            if turn == at:
                rows = half_rows - rows * (len(heavy) - 1)
            parts.append((bit, sent[bit], filled, rows))
            sent[bit] += rows
            filled += rows
        tiles.append((1, parts))
    return None, None, tiles, None


def flipped(index, mask):
    for k in range(16):
        if mask >> k & 1:
            step = 1 << k
            index = index + step * (1 - 2 * ((index // step) % 2))
    return index


def meet(bits, scale, low_count, *refs):
    (own_ref, match_ref, image_ref, text_ref, loss_ref, *refs) = refs
    (blocks, labels, logits, g, losses, own_sem, send_sem, recv_sem, near_sem) = refs
    _, half_rows, width = own_ref.shape
    near, far, tiles, passed = plan_for(bits, half_rows)
    pieces = half_rows // PIECE
    dx, dy = lax.axis_index("dx"), lax.axis_index("dy")

    def device(mask):
        return (flipped(dx, mask // low_count), flipped(dy, mask % low_count))

    masks = {bit: 1 << bit for bit in bits}
    if far is not None:
        masks[far] = 1 << near | 1 << far
    barrier = pltpu.get_barrier_semaphore()
    for bit in bits:
        pl.semaphore_signal(barrier, inc=1, device_id=device(masks[bit]), device_id_type=MESH)

    first_row = {(bit, half): 2 + k for k, (half, parts) in enumerate(tiles) for bit, *_ in parts}
    keep = pltpu.make_async_copy(own_ref, blocks.at[pl.ds(0, 2)], own_sem)
    keep.start()

    def part_copy(k, half, part):
        bit, start, row, rows = part
        return pltpu.make_async_remote_copy(
            src_ref=own_ref.at[half, pl.ds(start, rows)],
            dst_ref=blocks.at[k, pl.ds(row, rows)],
            send_sem=send_sem.at[k],
            recv_sem=recv_sem.at[k],
            device_id=device(masks[bit]),
            device_id_type=MESH,
        )

    def piece_copy(half, piece, forward):
        rows = pl.ds(pl.multiple_of(piece * PIECE, PIECE), PIECE)
        here = first_row[near, 0] + half * (first_row[near, 1] - first_row[near, 0])
        there = first_row[far, 0] + half * (first_row[far, 1] - first_row[far, 0])
        return pltpu.make_async_remote_copy(
            src_ref=blocks.at[here, rows] if forward else own_ref.at[half, rows],
            dst_ref=blocks.at[there if forward else here, rows],
            send_sem=send_sem.at[there if forward else here],
            recv_sem=recv_sem.at[there] if forward else near_sem.at[half, piece],
            device_id=device(masks[far if forward else near]),
            device_id_type=MESH,
        )

    pl.semaphore_wait(barrier, len(bits))
    sends = [
        (half, -LOAD[part[0]], part[1], k, part)
        for k, (half, parts) in enumerate(tiles, 2)
        for part in parts
        if part[0] not in (near, far)
    ]
    for half in (0, 1):
        if near is not None:

            @pl.loop(0, pieces)
            def _(piece, half=half):
                piece_copy(half, piece, False).start()

        for _, _, _, k, part in sorted(send for send in sends if send[0] == half):
            part_copy(k, half, part).start()

    @pl.loop(0, half_rows // ROWS)
    def _(step):
        rows = pl.ds(pl.multiple_of(step * ROWS, ROWS), ROWS)
        zero = jnp.zeros((ROWS, width), jnp.float32)
        image_ref[rows, :] = zero
        text_ref[rows, :] = zero

    square = (half_rows, half_rows)
    row = lax.broadcasted_iota(jnp.int32, square, 0)
    column = lax.broadcasted_iota(jnp.int32, square, 1)
    short = jnp.bfloat16
    hits = jnp.where(row == match_ref[...], 1.0, 0.0).astype(short)
    labels[1] = hits
    labels[0] = across(jnp.where(row == column, 1.0, 0.0).astype(short), hits).astype(short)
    labels[2] = jnp.zeros(square, short)
    losses[...] = jnp.zeros_like(losses)
    keep.wait()

    def chosen(k, numbers):
        return sum(((k == number).astype(jnp.int32) for number in numbers), jnp.int32(0))

    @pl.loop(0, 2 + len(tiles))
    def _(k):
        side = chosen(k, [1] + [at for at, (half, _) in enumerate(tiles, 2) if half == 1])

        if near is not None:
            low = sum((more - less) * (k > at).astype(jnp.int32) for at, (less, more) in enumerate(zip([0] + passed, passed)) if more > less)
            high = sum((more - less) * (k >= at).astype(jnp.int32) for at, (less, more) in enumerate(zip([0] + passed, passed)) if more > less)

            @pl.loop(low, high)
            def _(at):
                half = at // pieces
                piece = at - half * pieces
                piece_copy(half, piece, False).wait_recv()
                piece_copy(half, piece, True).start()

            waits = chosen(k, [at for at, (_, parts) in enumerate(tiles, 2) if parts[0][0] != near])
        else:
            waits = (k >= 2).astype(jnp.int32)

        @pl.when(waits == 1)
        def _():
            pltpu.make_async_copy(blocks.at[k], blocks.at[k], recv_sem.at[k]).wait()

        logits[...] = jnp.full(square, BIAS, jnp.float32)

        @pl.loop(0, width // WIDE)
        def _(step):
            columns = pl.ds(pl.multiple_of(step * WIDE, WIDE), WIDE)
            logits[...] += across(blocks[1 - side, :, columns], blocks[k, :, columns])

        @pl.loop(0, half_rows // ROWS)
        def _(step):
            rows = pl.ds(pl.multiple_of(step * ROWS, ROWS), ROWS)
            x = logits[rows, :]
            label = labels[jnp.minimum(k, 2), rows, :].astype(jnp.float32)
            e = jnp.exp(-jnp.abs(x))
            s = jnp.where(x >= 0, 1.0, e) / (1.0 + e)
            g[rows, :] = (s - label).astype(short)

        @pl.loop(0, (1 - side) * (half_rows // ROWS))
        def _(step):
            rows = pl.ds(pl.multiple_of(step * ROWS, ROWS), ROWS)
            x = logits[rows, :]
            label = labels[jnp.minimum(k, 2), rows, :].astype(jnp.float32)
            loss = jnp.maximum(jnp.where(label > 0, -x, x), 0.0) + jnp.log1p(jnp.exp(-jnp.abs(x)))
            losses[...] += jnp.sum(loss.reshape(ROWS // 8, 8, half_rows), axis=0)

        for number, grad_ref in enumerate((image_ref, text_ref)):

            @pl.loop(0, (side == number).astype(jnp.int32) * (width // WIDE))
            def _(step, grad_ref=grad_ref):
                columns = pl.ds(pl.multiple_of(step * WIDE, WIDE), WIDE)
                grad_ref[:, columns] += times(g[...], blocks[k, :, columns])

    loss_ref[0] = jnp.sum(losses[...]) * scale

    @pl.loop(2, 2 + len(tiles))
    def _(k):
        side = chosen(k, [at for at, (half, _) in enumerate(tiles, 2) if half == 1])
        pltpu.make_async_copy(own_ref.at[side], own_ref.at[side], send_sem.at[k]).wait()


def meet_call(bits, number, scale, low_count, own, match):
    _, half, width = own.shape
    places = 2 + 2 * len(bits)
    vmem = pl.BlockSpec(memory_space=pltpu.VMEM)
    return pl.pallas_call(
        partial(meet, bits, scale, low_count),
        out_shape=(
            pltpu.VMEM((half, width), jnp.float32),
            pltpu.VMEM((half, width), jnp.float32),
            jax.ShapeDtypeStruct((1,), jnp.float32),
        ),
        in_specs=[vmem, vmem],
        out_specs=(vmem, vmem, pl.BlockSpec(memory_space=pltpu.SMEM)),
        scratch_shapes=[
            pltpu.VMEM((places, half, width), jnp.bfloat16),
            pltpu.VMEM((3, half, half), jnp.bfloat16),
            pltpu.VMEM((half, half), jnp.float32),
            pltpu.VMEM((half, half), jnp.bfloat16),
            pltpu.VMEM((8, half), jnp.float32),
            pltpu.SemaphoreType.DMA,
            pltpu.SemaphoreType.DMA((places,)),
            pltpu.SemaphoreType.DMA((places,)),
            pltpu.SemaphoreType.DMA((2, half // PIECE)),
        ],
        compiler_params=pltpu.CompilerParams(
            collective_id=number, has_side_effects=True, vmem_limit_bytes=24 * 2**20
        ),
        cost_estimate=pl.CostEstimate(
            flops=32 * half * half * width, bytes_accessed=16 * half * width, transcendentals=0
        ),
        name="meet_" + "_".join(str(bit) for bit in bits),
    )(own, match)


def across(a, b):
    return lax.dot_general(a, b, (((1,), (1,)), ((), ())), preferred_element_type=jnp.float32)


def times(a, b):
    return jnp.dot(a, b, preferred_element_type=jnp.float32)


def prepare(all_bits, masks_ref, images_ref, texts_ref, own_ref, index_ref, wide, load_sem):
    half_rows = texts_ref.shape[0]
    loads = [
        (half, at, pltpu.make_async_copy(
            ref.at[pl.ds(at, ROWS)], wide.at[half, pl.ds(at, ROWS)], load_sem.at[half, at // ROWS]
        ))
        for half, ref in enumerate((texts_ref, images_ref))
        for at in range(0, half_rows, ROWS)
    ]
    for _, _, load in loads:
        load.start()
    first, third = masks_ref[0], masks_ref[2]
    low, high = jnp.minimum(first, third), jnp.maximum(first, third)
    low_bit, high_bit = jnp.int32(0), jnp.int32(0)
    for k in range(1, all_bits):
        low_bit += (low >= 1 << k).astype(jnp.int32)
        high_bit += (high >= 1 << k).astype(jnp.int32)
    before = low_bit * (all_bits - 1) - low_bit * (low_bit + 1) // 2
    index_ref[0] = before + high_bit - low_bit - 1
    for half, at, load in loads:
        load.wait()
        own_ref[half, pl.ds(at, ROWS), :] = wide[half, pl.ds(at, ROWS), :].astype(jnp.bfloat16)


def body(low_count, all_bits, images, texts, match, masks):
    low_bits = low_count.bit_length() - 1
    half, width = images.shape
    scale = 1.0 / (half * half * (masks.shape[0] + 1.0))
    smem = pl.BlockSpec(memory_space=pltpu.SMEM)
    anywhere = pl.BlockSpec(memory_space=pl.ANY)
    own, index = pl.pallas_call(
        partial(prepare, all_bits),
        out_shape=(pltpu.VMEM((2, half, width), jnp.bfloat16), pltpu.SMEM((1,), jnp.int32)),
        in_specs=[smem, anywhere, anywhere],
        out_specs=(pl.BlockSpec(memory_space=pltpu.VMEM), smem),
        scratch_shapes=[
            pltpu.VMEM((2, half, width), jnp.float32),
            pltpu.SemaphoreType.DMA((2, half // ROWS)),
        ],
        compiler_params=pltpu.CompilerParams(vmem_limit_bytes=16 * 2**20),
        name="prepare",
    )(*(pltpu.with_memory_space_constraint(x, pltpu.HBM) for x in (masks, images, texts)))
    sets = [
        (low, high, SECOND) for low in range(low_bits) for high in range(low + 1, all_bits - 1)
    ]
    branches = [
        partial(meet_call, bits, number, scale, low_count) for number, bits in enumerate(sets)
    ]
    return lax.switch(index[0], branches, own, match)


def solution(mesh):
    rows = P(("dx", "dy"), None)
    low_count = mesh.shape["dy"]
    all_bits = (low_count * mesh.shape["dx"]).bit_length() - 1
    return jax.shard_map(
        partial(body, low_count, all_bits),
        mesh=mesh,
        in_specs=(rows, rows, rows, P()),
        out_specs=(rows, rows, P(("dx", "dy"))),
        check_vma=False,
    )
```

time: 45.4 us -> 135 us (2.97)
  the two profiles are of different devices: /device:TPU:4 before, /device:TPU:88 now
where the time goes in v3:
time: 135 us
  Pallas kernels  130 us (96%)
  between operations  2.49 us (2%)
  local copies, waits for them, and re-layouts  2.03 us (2%)
    pallas_call x1, Pallas kernels, meet_call(): pl.pallas_call(partial(meet, bits, scale, low_count), out_shape=(pltpu.VM...  128 us

profile of v3, /device:TPU:88, one launch (start us, length us, event | category | flops | bytes accessed | tf_op | source)
XLA Modules:
  0.0 135.1 jit_solution(4520807413184099887)
XLA Ops:
  0.6 0.0 copy-start
  0.6 2.5 %prepare.1 = (bf16[2,256,1152]{2,1,0:T(8,128)(2,1)S(1)}, s32[1]{0:T(128)S(4)}) custom-call(s32[3]{0:T(128)} %masks_ref.1, f32[256,1152]{1,0:T(8,128)} %images_ref.1, f32[256,1152]{1,0:T(8,128)} %texts_ref.1), custom_call_target="tpu_custom_call" | custom-call | tf_op jit(solution)/shard_map/prepare/pallas_call | solution.py:281
  3.1 0.0 copy-done
  3.1 128.1 %conditional.1 = ((f32[256,1152]{1,0:T(8,128)S(1)}, f32[256,1152]{1,0:T(8,128)S(1)}, f32[1]{0:T(128)})) conditional(s32[]{:T(128)} %bitcast, (bf16[2,256,1152]{2,1,0:T(8,128)(2,1)S(1)}, s32[1,256]{1,0:T(1,128)S(1)}) %tuple.211, (bf16[2,256,1152]{2,1,0:T(8,128)(2,1)S(1)}, s32[1,256]{1,0:T(1,128)S(1)}) %tuple.212, ...), branch_computations={%region_0.0_spmd, %region_1.0_spmd, %region_2.0_spmd, %region_3.0_... | conditional | flops 2415919104 | bytes 4718600 | solution.py:299
  3.4 127.7 %meet_4_5_8.1 = (f32[256,1152]{1,0:T(8,128)S(1)}, f32[256,1152]{1,0:T(8,128)S(1)}, f32[1]{0:T(128)}) custom-call(bf16[2,256,1152]{2,1,0:T(8,128)(2,1)S(1)} %get-tuple-element.144.refs_0_, s32[1,256]{1,0:T(1,128)S(1)} %get-tuple-element.145.refs_1_), custom_call_target="tpu_custom_call" | custom-call | flops 2415919104 | bytes 4718592 | tf_op jit(solution)/shard_map/cond/branch_22_fun/meet_4_5_8/pallas_call | solution.py:213
  131.3 1.0 copy.160
  132.3 1.0 copy.161
Async XLA Ops:
  0.6 2.5 %copy-start = (s32[1,256]{1,0:T(1,128)S(1)}, s32[1,256]{1,0:T(1,128)}, u32[]{:S(2)}) copy-start(s32[1,256]{1,0:T(1,128)} %param.31) | copy-start | bytes 3076

commit v4 on v3

--- a/solution.py
+++ b/solution.py
@@ -13,6 +13,7 @@
 WIDE = 384
 ROWS = 64
 PIECE = 32
+STORES = 4
 
 LOAD = {0: 0.2, 1: 1, 2: 1.01, 3: 4, 4: 4.01, 5: 1, 6: 2, 7: 1, 8: 1.02}
 RELAYED = {(1, 2), (3, 4), (4, 5), (4, 6), (7, 8)}
@@ -61,9 +62,9 @@
 
 
 def meet(bits, scale, low_count, *refs):
-    (own_ref, match_ref, image_ref, text_ref, loss_ref, *refs) = refs
-    (blocks, labels, logits, g, losses, own_sem, send_sem, recv_sem, near_sem) = refs
-    _, half_rows, width = own_ref.shape
+    (own_ref, images_ref, match_ref, image_ref, text_ref, blocks, g, loss_ref, *refs) = refs
+    (wide, labels, logits, losses, own_sem, load_sem, send_sem, recv_sem, near_sem) = refs
+    half_rows, width = own_ref.shape
     near, far, tiles, passed = plan_for(bits, half_rows)
     pieces = half_rows // PIECE
     dx, dy = lax.axis_index("dx"), lax.axis_index("dy")
@@ -79,13 +80,22 @@
         pl.semaphore_signal(barrier, inc=1, device_id=device(masks[bit]), device_id_type=MESH)
 
     first_row = {(bit, half): 2 + k for k, (half, parts) in enumerate(tiles) for bit, *_ in parts}
-    keep = pltpu.make_async_copy(own_ref, blocks.at[pl.ds(0, 2)], own_sem)
+    keep = pltpu.make_async_copy(own_ref, blocks.at[0], own_sem)
     keep.start()
+    sources = (own_ref, blocks.at[1])
+
+    def load(step):
+        rows = pl.ds(pl.multiple_of(step * ROWS, ROWS), ROWS)
+        return rows, pltpu.make_async_copy(images_ref.at[rows], wide.at[rows], load_sem.at[step])
+
+    steps = half_rows // ROWS
+    for step in range(steps):
+        load(step)[1].start()
 
     def part_copy(k, half, part):
         bit, start, row, rows = part
         return pltpu.make_async_remote_copy(
-            src_ref=own_ref.at[half, pl.ds(start, rows)],
+            src_ref=sources[half].at[pl.ds(start, rows)],
             dst_ref=blocks.at[k, pl.ds(row, rows)],
             send_sem=send_sem.at[k],
             recv_sem=recv_sem.at[k],
@@ -96,9 +106,10 @@
     def piece_copy(half, piece, forward):
         rows = pl.ds(pl.multiple_of(piece * PIECE, PIECE), PIECE)
         here = first_row[near, 0] + half * (first_row[near, 1] - first_row[near, 0])
+        source = blocks.at[here] if forward else sources[half] if isinstance(half, int) else own_ref
         there = first_row[far, 0] + half * (first_row[far, 1] - first_row[far, 0])
         return pltpu.make_async_remote_copy(
-            src_ref=blocks.at[here, rows] if forward else own_ref.at[half, rows],
+            src_ref=source.at[rows],
             dst_ref=blocks.at[there if forward else here, rows],
             send_sem=send_sem.at[there if forward else here],
             recv_sem=recv_sem.at[there] if forward else near_sem.at[half, piece],
@@ -114,6 +125,14 @@
         if part[0] not in (near, far)
     ]
     for half in (0, 1):
+        if half == 1:
+
+            @pl.loop(0, steps)
+            def _(step):
+                rows, arriving = load(step)
+                arriving.wait()
+                blocks[1, rows, :] = wide[rows, :].astype(jnp.bfloat16)
+
         if near is not None:
 
             @pl.loop(0, pieces)
@@ -123,7 +142,7 @@
         for _, _, _, k, part in sorted(send for send in sends if send[0] == half):
             part_copy(k, half, part).start()
 
-    @pl.loop(0, half_rows // ROWS)
+    @pl.loop(0, steps)
     def _(step):
         rows = pl.ds(pl.multiple_of(step * ROWS, ROWS), ROWS)
         zero = jnp.zeros((ROWS, width), jnp.float32)
@@ -163,11 +182,15 @@
         else:
             waits = (k >= 2).astype(jnp.int32)
 
+        logits[...] = jnp.full(square, BIAS, jnp.float32)
+
+        @pl.when(k > len(tiles))
+        def _():
+            loss_ref[0] = jnp.sum(losses[...]) * scale
+
         @pl.when(waits == 1)
         def _():
             pltpu.make_async_copy(blocks.at[k], blocks.at[k], recv_sem.at[k]).wait()
-
-        logits[...] = jnp.full(square, BIAS, jnp.float32)
 
         @pl.loop(0, width // WIDE)
         def _(step):
@@ -192,22 +215,20 @@
             losses[...] += jnp.sum(loss.reshape(ROWS // 8, 8, half_rows), axis=0)
 
         for number, grad_ref in enumerate((image_ref, text_ref)):
-
-            @pl.loop(0, (side == number).astype(jnp.int32) * (width // WIDE))
+            now = jnp.logical_and(side == number, k <= len(tiles)).astype(jnp.int32)
+
+            @pl.loop(0, now * (width // WIDE))
             def _(step, grad_ref=grad_ref):
                 columns = pl.ds(pl.multiple_of(step * WIDE, WIDE), WIDE)
                 grad_ref[:, columns] += times(g[...], blocks[k, :, columns])
 
-    loss_ref[0] = jnp.sum(losses[...]) * scale
-
     @pl.loop(2, 2 + len(tiles))
     def _(k):
-        side = chosen(k, [at for at, (half, _) in enumerate(tiles, 2) if half == 1])
-        pltpu.make_async_copy(own_ref.at[side], own_ref.at[side], send_sem.at[k]).wait()
-
-
-def meet_call(bits, number, scale, low_count, own, match):
-    _, half, width = own.shape
+        pltpu.make_async_copy(own_ref, own_ref, send_sem.at[k]).wait()
+
+
+def meet_call(bits, number, scale, low_count, own, images, match):
+    half, width = own.shape
     places = 2 + 2 * len(bits)
     vmem = pl.BlockSpec(memory_space=pltpu.VMEM)
     return pl.pallas_call(
@@ -215,17 +236,19 @@
         out_shape=(
             pltpu.VMEM((half, width), jnp.float32),
             pltpu.VMEM((half, width), jnp.float32),
+            pltpu.VMEM((places, half, width), jnp.bfloat16),
+            pltpu.VMEM((half, half), jnp.bfloat16),
             jax.ShapeDtypeStruct((1,), jnp.float32),
         ),
-        in_specs=[vmem, vmem],
-        out_specs=(vmem, vmem, pl.BlockSpec(memory_space=pltpu.SMEM)),
+        in_specs=[vmem, pl.BlockSpec(memory_space=pl.ANY), vmem],
+        out_specs=(vmem, vmem, vmem, vmem, pl.BlockSpec(memory_space=pltpu.SMEM)),
         scratch_shapes=[
-            pltpu.VMEM((places, half, width), jnp.bfloat16),
+            pltpu.VMEM((half, width), jnp.float32),
             pltpu.VMEM((3, half, half), jnp.bfloat16),
             pltpu.VMEM((half, half), jnp.float32),
-            pltpu.VMEM((half, half), jnp.bfloat16),
             pltpu.VMEM((8, half), jnp.float32),
             pltpu.SemaphoreType.DMA,
+            pltpu.SemaphoreType.DMA((half // ROWS,)),
             pltpu.SemaphoreType.DMA((places,)),
             pltpu.SemaphoreType.DMA((places,)),
             pltpu.SemaphoreType.DMA((2, half // PIECE)),
@@ -237,7 +260,49 @@
             flops=32 * half * half * width, bytes_accessed=16 * half * width, transcendentals=0
         ),
         name="meet_" + "_".join(str(bit) for bit in bits),
-    )(own, match)
+    )(own, images, match)
+
+
+def finish(image_ref, text_ref, blocks, g, image_out, text_out, ready, store_sem):
+    half_rows, width = image_ref.shape
+    rows = half_rows // STORES
+    stores = [
+        pltpu.make_async_copy(
+            image_ref.at[pl.ds(at * rows, rows)], image_out.at[pl.ds(at * rows, rows)], store_sem.at[at]
+        )
+        for at in range(STORES)
+    ]
+    for store in stores:
+        store.start()
+    for at in range(width // WIDE):
+        columns = pl.ds(at * WIDE, WIDE)
+        ready[:, columns] = text_ref[:, columns] + times(g[...], blocks[blocks.shape[0] - 1, :, columns])
+        store = pltpu.make_async_copy(
+            ready.at[:, columns], text_out.at[:, columns], store_sem.at[STORES + at]
+        )
+        store.start()
+        stores.append(store)
+    for store in stores:
+        store.wait()
+
+
+def finish_call(image, text, blocks, g):
+    half, width = image.shape
+    grad = jax.ShapeDtypeStruct((half, width), jnp.float32)
+    vmem = pl.BlockSpec(memory_space=pltpu.VMEM)
+    anywhere = pl.BlockSpec(memory_space=pl.ANY)
+    return pl.pallas_call(
+        finish,
+        out_shape=(grad, grad),
+        in_specs=[anywhere, vmem, vmem, vmem],
+        out_specs=(anywhere, anywhere),
+        scratch_shapes=[
+            pltpu.VMEM((half, width), jnp.float32),
+            pltpu.SemaphoreType.DMA((STORES + width // WIDE,)),
+        ],
+        compiler_params=pltpu.CompilerParams(vmem_limit_bytes=16 * 2**20),
+        name="finish",
+    )(image, text, blocks, g)
 
 
 def across(a, b):
@@ -248,16 +313,14 @@
     return jnp.dot(a, b, preferred_element_type=jnp.float32)
 
 
-def prepare(all_bits, masks_ref, images_ref, texts_ref, own_ref, index_ref, wide, load_sem):
-    half_rows = texts_ref.shape[0]
+def prepare(all_bits, masks_ref, texts_ref, own_ref, index_ref, wide, load_sem):
     loads = [
-        (half, at, pltpu.make_async_copy(
-            ref.at[pl.ds(at, ROWS)], wide.at[half, pl.ds(at, ROWS)], load_sem.at[half, at // ROWS]
-        ))
-        for half, ref in enumerate((texts_ref, images_ref))
-        for at in range(0, half_rows, ROWS)
-    ]
-    for _, _, load in loads:
+        pltpu.make_async_copy(
+            texts_ref.at[pl.ds(at, ROWS)], wide.at[pl.ds(at, ROWS)], load_sem.at[at // ROWS]
+        )
+        for at in range(0, texts_ref.shape[0], ROWS)
+    ]
+    for load in loads:
         load.start()
     first, third = masks_ref[0], masks_ref[2]
     low, high = jnp.minimum(first, third), jnp.maximum(first, third)
@@ -267,36 +330,40 @@
         high_bit += (high >= 1 << k).astype(jnp.int32)
     before = low_bit * (all_bits - 1) - low_bit * (low_bit + 1) // 2
     index_ref[0] = before + high_bit - low_bit - 1
-    for half, at, load in loads:
+    for at, load in enumerate(loads):
         load.wait()
-        own_ref[half, pl.ds(at, ROWS), :] = wide[half, pl.ds(at, ROWS), :].astype(jnp.bfloat16)
+        rows = pl.ds(at * ROWS, ROWS)
+        own_ref[rows, :] = wide[rows, :].astype(jnp.bfloat16)
 
 
 def body(low_count, all_bits, images, texts, match, masks):
     low_bits = low_count.bit_length() - 1
     half, width = images.shape
     scale = 1.0 / (half * half * (masks.shape[0] + 1.0))
+    images, texts, masks = (
+        pltpu.with_memory_space_constraint(x, pltpu.HBM) for x in (images, texts, masks)
+    )
     smem = pl.BlockSpec(memory_space=pltpu.SMEM)
-    anywhere = pl.BlockSpec(memory_space=pl.ANY)
     own, index = pl.pallas_call(
         partial(prepare, all_bits),
-        out_shape=(pltpu.VMEM((2, half, width), jnp.bfloat16), pltpu.SMEM((1,), jnp.int32)),
-        in_specs=[smem, anywhere, anywhere],
+        out_shape=(pltpu.VMEM((half, width), jnp.bfloat16), pltpu.SMEM((1,), jnp.int32)),
+        in_specs=[smem, pl.BlockSpec(memory_space=pl.ANY)],
         out_specs=(pl.BlockSpec(memory_space=pltpu.VMEM), smem),
         scratch_shapes=[
-            pltpu.VMEM((2, half, width), jnp.float32),
-            pltpu.SemaphoreType.DMA((2, half // ROWS)),
+            pltpu.VMEM((half, width), jnp.float32),
+            pltpu.SemaphoreType.DMA((half // ROWS,)),
         ],
         compiler_params=pltpu.CompilerParams(vmem_limit_bytes=16 * 2**20),
         name="prepare",
-    )(*(pltpu.with_memory_space_constraint(x, pltpu.HBM) for x in (masks, images, texts)))
+    )(masks, texts)
     sets = [
         (low, high, SECOND) for low in range(low_bits) for high in range(low + 1, all_bits - 1)
     ]
     branches = [
         partial(meet_call, bits, number, scale, low_count) for number, bits in enumerate(sets)
     ]
-    return lax.switch(index[0], branches, own, match)
+    *terms, loss = lax.switch(index[0], branches, own, images, match)
+    return (*finish_call(*terms), loss)
 
 
 def solution(mesh):

time: 135 us -> 131 us (0.970)
  the two profiles are of different devices: /device:TPU:88 before, /device:TPU:38 now
where the time goes in v4:
time: 131 us
  Pallas kernels  126 us (96%)
  between operations  2.41 us (2%)
  local copies, waits for them, and re-layouts  2.17 us (2%)
    pallas_call x1, Pallas kernels, meet_call(): pl.pallas_call(partial(meet, bits, scale, low_count), out_shape=(pltpu.VM...  121 us
    pallas_call x1, Pallas kernels, finish_call(): pl.pallas_call(finish, out_shape=(grad, grad), in_specs=[anywhere, vmem,...  3.81 us

profile of v4, /device:TPU:38, one launch (start us, length us, event | category | flops | bytes accessed | tf_op | source)
XLA Modules:
  0.0 131.1 jit_solution(5735907990185520992)
XLA Ops:
  0.6 0.0 copy-start.25
  0.6 2.1 %prepare.1 = (bf16[256,1152]{1,0:T(8,128)(2,1)S(1)}, s32[1]{0:T(128)S(4)}) custom-call(s32[3]{0:T(128)} %masks_ref.1, f32[256,1152]{1,0:T(8,128)} %texts_ref.1), custom_call_target="tpu_custom_call" | custom-call | tf_op jit(solution)/shard_map/prepare/pallas_call | solution.py:347
  2.7 0.0 copy-done.25
  2.7 122.8 %conditional.1 = ((f32[256,1152]{1,0:T(8,128)S(1)}, f32[256,1152]{1,0:T(8,128)S(1)}, bf16[8,256,1152]{2,1,0:T(8,128)(2,1)}, bf16[256,256]{1,0:T(8,128)(2,1)S(1)}, f32[1]{0:T(128)})) conditional(s32[]{:T(128)} %bitcast, (bf16[256,1152]{1,0:T(8,128)(2,1)S(1)}, f32[256,1152]{1,0:T(8,128)}, ...), branch_computations={%region_0.0_spmd, %region_1.0_spmd, %region_2.0_spmd, %region_3.0_... | conditional | flops 2415919104 | bytes 23593036 | solution.py:365
  2.8 120.6 %meet_1_4_8.1 = (f32[256,1152]{1,0:T(8,128)S(1)}, f32[256,1152]{1,0:T(8,128)S(1)}, bf16[8,256,1152]{2,1,0:T(8,128)(2,1)S(1)}, bf16[256,256]{1,0:T(8,128)(2,1)S(1)}, f32[1]{0:T(128)}) custom-call(bf16[256,1152]{1,0:T(8,128)(2,1)S(1)} %get-tuple-element.177.refs_0_, f32[256,1152]{1,0:T(8,128)} %get-tuple-element.178.refs_1_, ...), custom_call_target="tpu_custom_call" | custom-call | flops 2415919104 | bytes 4718592 | tf_op jit(solution)/shard_map/cond/branch_9_fun/meet_1_4_8/pallas_call | solution.py:234
  123.4 0.0 copy-start.9
  123.4 2.2 %copy-done.9 = bf16[8,256,1152]{2,1,0:T(8,128)(2,1)} copy-done((bf16[8,256,1152]{2,1,0:T(8,128)(2,1)}, bf16[8,256,1152]{2,1,0:T(8,128)(2,1)S(1)}, u32[]{:S(2)}) %copy-start.9) | copy-done | bytes 4718616 | tf_op jit(solution)/shard_map/cond
  125.6 3.8 %finish.1 = (f32[256,1152]{1,0:T(8,128)}, f32[256,1152]{1,0:T(8,128)}) custom-call(f32[256,1152]{1,0:T(8,128)S(1)} %get-tuple-element.239.image_ref, f32[256,1152]{1,0:T(8,128)S(1)} %get-tuple-element.240.text_ref, bf16[8,256,1152]{2,1,0:T(8,128)(2,1)} %get-tuple-element.241.blocks, bf16[256,256]{1,0:T(8,128)(2,1)S(1)} %get-tuple-element.242.g), custom_call_target="tpu_custom_call" | custom-call | tf_op jit(solution)/shard_map/finish/pallas_call | solution.py:294
Async XLA Ops:
  0.6 2.1 %copy-start.25 = (s32[1,256]{1,0:T(1,128)S(1)}, s32[1,256]{1,0:T(1,128)}, u32[]{:S(2)}) copy-start(s32[1,256]{1,0:T(1,128)} %param.31) | copy-start | bytes 3076
  123.4 2.2 %copy-start.9 = (bf16[8,256,1152]{2,1,0:T(8,128)(2,1)}, bf16[8,256,1152]{2,1,0:T(8,128)(2,1)S(1)}, u32[]{:S(2)}) copy-start(bf16[8,256,1152]{2,1,0:T(8,128)(2,1)S(1)} %get-tuple-element.423) | copy-start | bytes 14155780 | tf_op jit(solution)/shard_map/cond

commit v5 on v3

--- a/solution.py
+++ b/solution.py
@@ -15,6 +15,7 @@
 PIECE = 32
 
 LOAD = {0: 0.2, 1: 1, 2: 1.01, 3: 4, 4: 4.01, 5: 1, 6: 2, 7: 1, 8: 1.02}
+HALFWAY, NEIGHBOUR = 4, 5
 RELAYED = {(1, 2), (3, 4), (4, 5), (4, 6), (7, 8)}
 
 
@@ -23,18 +24,22 @@
         return half, [(bit, 0, 0, half_rows)]
 
     order = sorted(bits, key=lambda bit: LOAD[bit])
+    pieces = half_rows // PIECE
     for pair in RELAYED:
         if set(pair) <= set(bits) and LOAD[order[-1]] < 2 * max(LOAD[bit] for bit in pair):
             near, far = sorted(pair, key=lambda bit: LOAD[bit])
             (other,) = set(bits) - set(pair)
-            pieces = half_rows // PIECE
             if LOAD[other] * 2 < LOAD[far]:
-                uses = [(other, 0), (other, 1), (near, 0), (far, 0), (near, 1), (far, 1)]
-                passed = [0, 0, pieces // 4, pieces // 2, pieces, pieces * 3 // 2, 2 * pieces, 2 * pieces]
+                uses = [(other, 0), (near, 0), (other, 1), (far, 0), (near, 1), (far, 1)]
+                passed = [1, 2, 4, pieces, pieces + 4, pieces + 6, 2 * pieces, 2 * pieces]
             else:
                 uses = [(near, 0), (other, 0), (far, 0), (near, 1), (other, 1), (far, 1)]
-                passed = [0, 0, pieces, pieces * 5 // 4, pieces * 3 // 2, 2 * pieces, 2 * pieces, 2 * pieces]
+                passed = [1, 2, pieces, pieces + 2, pieces + 4, 2 * pieces, 2 * pieces, 2 * pieces]
             return near, far, [whole(*use) for use in uses], passed
+    if order[-1] == HALFWAY:
+        uses = [(bit, half) for part in (order[:-1], order[-1:]) for half in (0, 1) for bit in part]
+        passed = [1, 2, 6, pieces, pieces + 4, pieces + 6, 2 * pieces, 2 * pieces]
+        return NEIGHBOUR, HALFWAY, [whole(*use) for use in uses], passed
     light = [bit for bit in order if LOAD[bit] * 3 <= LOAD[order[-1]]]
     heavy = [bit for bit in order if bit not in light]
     tiles = [whole(bit, half) for bit in light for half in (0, 1)] + [whole(bit, 0) for bit in heavy]
@@ -62,7 +67,7 @@
 
 def meet(bits, scale, low_count, *refs):
     (own_ref, match_ref, image_ref, text_ref, loss_ref, *refs) = refs
-    (blocks, labels, logits, g, losses, own_sem, send_sem, recv_sem, near_sem) = refs
+    (blocks, relay, labels, logits, g, losses, own_sem, send_sem, recv_sem, relay_sem, near_sem) = refs
     _, half_rows, width = own_ref.shape
     near, far, tiles, passed = plan_for(bits, half_rows)
     pieces = half_rows // PIECE
@@ -73,10 +78,11 @@
 
     masks = {bit: 1 << bit for bit in bits}
     if far is not None:
+        masks[near] = 1 << near
         masks[far] = 1 << near | 1 << far
     barrier = pltpu.get_barrier_semaphore()
-    for bit in bits:
-        pl.semaphore_signal(barrier, inc=1, device_id=device(masks[bit]), device_id_type=MESH)
+    for mask in masks.values():
+        pl.semaphore_signal(barrier, inc=1, device_id=device(mask), device_id_type=MESH)
 
     first_row = {(bit, half): 2 + k for k, (half, parts) in enumerate(tiles) for bit, *_ in parts}
     keep = pltpu.make_async_copy(own_ref, blocks.at[pl.ds(0, 2)], own_sem)
@@ -95,18 +101,22 @@
 
     def piece_copy(half, piece, forward):
         rows = pl.ds(pl.multiple_of(piece * PIECE, PIECE), PIECE)
-        here = first_row[near, 0] + half * (first_row[near, 1] - first_row[near, 0])
         there = first_row[far, 0] + half * (first_row[far, 1] - first_row[far, 0])
+        if near in bits:
+            here = first_row[near, 0] + half * (first_row[near, 1] - first_row[near, 0])
+            stop, sent = blocks.at[here, rows], send_sem.at[here]
+        else:
+            stop, sent = relay.at[half, rows], relay_sem.at[half]
         return pltpu.make_async_remote_copy(
-            src_ref=blocks.at[here, rows] if forward else own_ref.at[half, rows],
-            dst_ref=blocks.at[there if forward else here, rows],
-            send_sem=send_sem.at[there if forward else here],
+            src_ref=stop if forward else own_ref.at[half, rows],
+            dst_ref=blocks.at[there, rows] if forward else stop,
+            send_sem=send_sem.at[there] if forward else sent,
             recv_sem=recv_sem.at[there] if forward else near_sem.at[half, piece],
             device_id=device(masks[far if forward else near]),
             device_id_type=MESH,
         )
 
-    pl.semaphore_wait(barrier, len(bits))
+    pl.semaphore_wait(barrier, len(masks))
     sends = [
         (half, -LOAD[part[0]], part[1], k, part)
         for k, (half, parts) in enumerate(tiles, 2)
@@ -163,11 +173,15 @@
         else:
             waits = (k >= 2).astype(jnp.int32)
 
+        logits[...] = jnp.full(square, BIAS, jnp.float32)
+
+        @pl.when(k > len(tiles))
+        def _():
+            loss_ref[0] = jnp.sum(losses[...]) * scale
+
         @pl.when(waits == 1)
         def _():
             pltpu.make_async_copy(blocks.at[k], blocks.at[k], recv_sem.at[k]).wait()
-
-        logits[...] = jnp.full(square, BIAS, jnp.float32)
 
         @pl.loop(0, width // WIDE)
         def _(step):
@@ -198,12 +212,13 @@
                 columns = pl.ds(pl.multiple_of(step * WIDE, WIDE), WIDE)
                 grad_ref[:, columns] += times(g[...], blocks[k, :, columns])
 
-    loss_ref[0] = jnp.sum(losses[...]) * scale
-
     @pl.loop(2, 2 + len(tiles))
     def _(k):
-        side = chosen(k, [at for at, (half, _) in enumerate(tiles, 2) if half == 1])
-        pltpu.make_async_copy(own_ref.at[side], own_ref.at[side], send_sem.at[k]).wait()
+        pltpu.make_async_copy(own_ref.at[0], own_ref.at[0], send_sem.at[k]).wait()
+
+    if near is not None and near not in bits:
+        for half in (0, 1):
+            pltpu.make_async_copy(own_ref.at[half], own_ref.at[half], relay_sem.at[half]).wait()
 
 
 def meet_call(bits, number, scale, low_count, own, match):
@@ -221,6 +236,7 @@
         out_specs=(vmem, vmem, pl.BlockSpec(memory_space=pltpu.SMEM)),
         scratch_shapes=[
             pltpu.VMEM((places, half, width), jnp.bfloat16),
+            pltpu.VMEM((2, half, width), jnp.bfloat16),
             pltpu.VMEM((3, half, half), jnp.bfloat16),
             pltpu.VMEM((half, half), jnp.float32),
             pltpu.VMEM((half, half), jnp.bfloat16),
@@ -228,6 +244,7 @@
             pltpu.SemaphoreType.DMA,
             pltpu.SemaphoreType.DMA((places,)),
             pltpu.SemaphoreType.DMA((places,)),
+            pltpu.SemaphoreType.DMA((2,)),
             pltpu.SemaphoreType.DMA((2, half // PIECE)),
         ],
         compiler_params=pltpu.CompilerParams(

time: 135 us -> 132 us (0.978)
  the two profiles are of different devices: /device:TPU:88 before, /device:TPU:1 now
where the time goes in v5:
time: 132 us; the launch traced here: 130 us
  Pallas kernels  125 us (95%)
  between operations  2.49 us (2%)
  local copies, waits for them, and re-layouts  2.03 us (2%)
    pallas_call x1, Pallas kernels, meet_call(): pl.pallas_call(partial(meet, bits, scale, low_count), out_shape=(pltpu.VM...  123 us

profile of v5, /device:TPU:1, one launch (start us, length us, event | category | flops | bytes accessed | tf_op | source)
XLA Modules:
  0.0 130.0 jit_solution(6135186384221326633)
XLA Ops:
  0.6 0.0 copy-start
  0.6 2.5 %prepare.1 = (bf16[2,256,1152]{2,1,0:T(8,128)(2,1)S(1)}, s32[1]{0:T(128)S(4)}) custom-call(s32[3]{0:T(128)} %masks_ref.1, f32[256,1152]{1,0:T(8,128)} %images_ref.1, f32[256,1152]{1,0:T(8,128)} %texts_ref.1), custom_call_target="tpu_custom_call" | custom-call | tf_op jit(solution)/shard_map/prepare/pallas_call | solution.py:298
  3.1 0.0 copy-done
  3.1 123.0 %conditional.1 = ((f32[256,1152]{1,0:T(8,128)S(1)}, f32[256,1152]{1,0:T(8,128)S(1)}, f32[1]{0:T(128)})) conditional(s32[]{:T(128)} %bitcast, (bf16[2,256,1152]{2,1,0:T(8,128)(2,1)S(1)}, s32[1,256]{1,0:T(1,128)S(1)}) %tuple.211, (bf16[2,256,1152]{2,1,0:T(8,128)(2,1)S(1)}, s32[1,256]{1,0:T(1,128)S(1)}) %tuple.212, ...), branch_computations={%region_0.0_spmd, %region_1.0_spmd, %region_2.0_spmd, %region_3.0_... | conditional | flops 2415919104 | bytes 4718600 | solution.py:316
  3.4 122.8 %meet_4_7_8.1 = (f32[256,1152]{1,0:T(8,128)S(1)}, f32[256,1152]{1,0:T(8,128)S(1)}, f32[1]{0:T(128)}) custom-call(bf16[2,256,1152]{2,1,0:T(8,128)(2,1)S(1)} %get-tuple-element.148.refs_0_, s32[1,256]{1,0:T(1,128)S(1)} %get-tuple-element.149.refs_1_), custom_call_target="tpu_custom_call" | custom-call | flops 2415919104 | bytes 4718592 | tf_op jit(solution)/shard_map/cond/branch_24_fun/meet_4_7_8/pallas_call | solution.py:228
  126.2 1.0 copy.160
  127.2 1.0 copy.161
Async XLA Ops:
  0.6 2.5 %copy-start = (s32[1,256]{1,0:T(1,128)S(1)}, s32[1,256]{1,0:T(1,128)}, u32[]{:S(2)}) copy-start(s32[1,256]{1,0:T(1,128)} %param.31) | copy-start | bytes 3076

commit v6 on v5

--- a/solution.py
+++ b/solution.py
@@ -16,6 +16,7 @@
 
 LOAD = {0: 0.2, 1: 1, 2: 1.01, 3: 4, 4: 4.01, 5: 1, 6: 2, 7: 1, 8: 1.02}
 HALFWAY, NEIGHBOUR = 4, 5
+QUARTER, TURN = 3, 6
 RELAYED = {(1, 2), (3, 4), (4, 5), (4, 6), (7, 8)}
 
 
@@ -116,6 +117,9 @@
             device_id_type=MESH,
         )
 
+    block = dx * low_count + dy
+    second = (block // (1 << QUARTER)) % 2 == (block // (1 << TURN)) % 2
+    turns = QUARTER in bits and near is None
     pl.semaphore_wait(barrier, len(masks))
     sends = [
         (half, -LOAD[part[0]], part[1], k, part)
@@ -131,7 +135,14 @@
                 piece_copy(half, piece, False).start()
 
         for _, _, _, k, part in sorted(send for send in sends if send[0] == half):
-            part_copy(k, half, part).start()
+            if turns and part[0] == QUARTER:
+
+                @pl.when(jnp.logical_not(second))
+                def _(k=k, half=half, part=part):
+                    part_copy(k, half, part).start()
+
+            else:
+                part_copy(k, half, part).start()
 
     @pl.loop(0, half_rows // ROWS)
     def _(step):
@@ -182,6 +193,14 @@
         @pl.when(waits == 1)
         def _():
             pltpu.make_async_copy(blocks.at[k], blocks.at[k], recv_sem.at[k]).wait()
+
+        if turns:
+
+            @pl.when(jnp.logical_and(second, k > len(tiles)))
+            def _():
+                for half, _, _, place, part in sends:
+                    if part[0] == QUARTER:
+                        part_copy(place, half, part).start()
 
         @pl.loop(0, width // WIDE)
         def _(step):

time: 132 us -> 132 us (level)
  no operation moved by 1% of the time
where the time goes in v6:
time: 132 us; the launch traced here: 130 us
  Pallas kernels  126 us (95%)
  between operations  2.49 us (2%)
  local copies, waits for them, and re-layouts  2.03 us (2%)
    pallas_call x1, Pallas kernels, meet_call(): pl.pallas_call(partial(meet, bits, scale, low_count), out_shape=(pltpu.VM...  123 us

profile of v6, /device:TPU:1, one launch (start us, length us, event | category | flops | bytes accessed | tf_op | source)
XLA Modules:
  0.0 130.3 jit_solution(13568832754586504299)
XLA Ops:
  0.6 0.0 copy-start
  0.6 2.5 %prepare.1 = (bf16[2,256,1152]{2,1,0:T(8,128)(2,1)S(1)}, s32[1]{0:T(128)S(4)}) custom-call(s32[3]{0:T(128)} %masks_ref.1, f32[256,1152]{1,0:T(8,128)} %images_ref.1, f32[256,1152]{1,0:T(8,128)} %texts_ref.1), custom_call_target="tpu_custom_call" | custom-call | tf_op jit(solution)/shard_map/prepare/pallas_call | solution.py:317
  3.1 0.0 copy-done
  3.1 123.3 %conditional.1 = ((f32[256,1152]{1,0:T(8,128)S(1)}, f32[256,1152]{1,0:T(8,128)S(1)}, f32[1]{0:T(128)})) conditional(s32[]{:T(128)} %bitcast, (bf16[2,256,1152]{2,1,0:T(8,128)(2,1)S(1)}, s32[1,256]{1,0:T(1,128)S(1)}) %tuple.211, (bf16[2,256,1152]{2,1,0:T(8,128)(2,1)S(1)}, s32[1,256]{1,0:T(1,128)S(1)}) %tuple.212, ...), branch_computations={%region_0.0_spmd, %region_1.0_spmd, %region_2.0_spmd, %region_3.0_... | conditional | flops 2415919104 | bytes 4718600 | solution.py:335
  3.4 123.1 %meet_2_4_8.1 = (f32[256,1152]{1,0:T(8,128)S(1)}, f32[256,1152]{1,0:T(8,128)S(1)}, f32[1]{0:T(128)}) custom-call(bf16[2,256,1152]{2,1,0:T(8,128)(2,1)S(1)} %get-tuple-element.128.refs_0_, s32[1,256]{1,0:T(1,128)S(1)} %get-tuple-element.129.refs_1_), custom_call_target="tpu_custom_call" | custom-call | flops 2415919104 | bytes 4718592 | tf_op jit(solution)/shard_map/cond/branch_14_fun/meet_2_4_8/pallas_call | solution.py:247
  126.5 1.0 copy.160
  127.5 1.0 copy.161
Async XLA Ops:
  0.6 2.5 %copy-start = (s32[1,256]{1,0:T(1,128)S(1)}, s32[1,256]{1,0:T(1,128)}, u32[]{:S(2)}) copy-start(s32[1,256]{1,0:T(1,128)} %param.31) | copy-start | bytes 3076
